TPU v7x, 32 devices: a whole 2x2x4 slice. The times are simulated.
32 devices in a mesh: runs: 2 (over y), gx: 16 (over z, x, core).
Axes of the slice: x: 2, y: 2, z: 4, core: 2. Of those that a mesh axis runs over, the one named last changes fastest.
Arguments:
- velocity: float32 [6, 64, 128, 128], P('runs', 'gx'), parts along dimension 0, may hold values from -4 to 4
- inflow: float32 [6, 128, 128], P('runs', 'gx'), parts along dimension 0, may hold values from -4 to 4
- blade_motion: float32 [6, 3072], P('runs', 'gx'), parts along dimension 0, may hold values from -6 to 6
- blade_axis: float32 [6, 3072], P('runs', 'gx'), parts along dimension 0, may hold values from -1 to 1
- blade_chord: float32 [6144], P(('runs', 'gx')), parts along dimension 0, may hold values from 0.3 to 1.5
- host_cell: int32 [6144], P(('runs', 'gx')), parts along dimension 0, may hold values from -1 to 49150, as said below
- host_frac: float32 [6, 3072], P('runs', 'gx'), parts along dimension 0, may hold values from 0 to 1
Outputs:
- new_velocity: float32 [6, 64, 128, 128], P('runs', 'gx'), parts along dimension 0
There are 2 independent parts, one for each index of `runs`. A program takes and returns all parts, laid end to end along the dimension named above; each array names one. Nothing has to cross between parts.
Inputs may be any that keep to these rules, and one draw needn't show every extreme that they name: `host_cell`: each tile's slots form 16 blocks of 12, block o for blade points owned by device o; slot o * 12 + c of tile t holds owner o's blade point t * 12 + c (that point's data are unused where the slot is empty). Blade points are assigned to owners without regard to their position. A quarter of all tiles are rotor tiles; occupied slots lie only in tiles whose index differs from some rotor tile's by at most one. An occupied slot's cell has streamwise index at most 2 and vertical index at most 126 within its tile. Empty slots may stand anywhere. In every draw some owner's block is full in every tile within one of some rotor tile.
All inputs are finite; a program needn't handle non-finite values.
Results may differ from a plain program's by a relative error of at most 0.00002.
Values sent between devices are 32-bit elements; how exact they have to be, the bound alone decides.
A program may use at most 128 MiB of HBM per device.

v0:
```python
import jax
import jax.numpy as jnp
from jax import lax
from jax.sharding import PartitionSpec as P

JACOBI = 3


TIME_STEP = 0.2
SMAGORINSKY = 0.0289
STRAIN_FLOOR = 0.01
FORCE_SCALE = 0.2


def padded_2(value, sides, width):
    for axis, dim in sides:
        size, length = (lax.axis_size(axis), value.shape[dim])
        up = [(i, (i + 1) % size) for i in range(size - 1)]
        down = [(j, i) for i, j in up]
        last = lax.slice_in_dim(value, length - width, length, axis=dim)
        initial = lax.slice_in_dim(value, 0, width, axis=dim)
        before = lax.ppermute(last, axis, up)
        after = lax.ppermute(initial, axis, down)
        value = jnp.concatenate([before, value, after], axis=dim)
    return value


def pad_depth(values, margin):
    spec = [(0, 0)] * (values.ndim - 1) + [(margin, margin)]
    return jnp.pad(values, spec)


def roll_span(values, shift_by):
    return jnp.roll(values, shift_by, axis=-2)


def tensor_of(padded):
    grad_x = 0.5 * (padded[:, 2:, :, 1:-1] - padded[:, :-2, :, 1:-1])
    middle = padded[:, 1:-1, :, 1:-1]
    grad_y = 0.5 * (roll_span(middle, -1) - roll_span(middle, 1))
    grad_z = 0.5 * (padded[:, 1:-1, :, 2:] - padded[:, 1:-1, :, :-2])
    return [[grad_x[comp], grad_y[comp], grad_z[comp]] for comp in range(3)]


def eddy_viscosity(table):
    shear_sum = jnp.zeros_like(table[0][0])
    for row_i in range(3):
        for col_j in range(3):
            pair_sum = table[row_i][col_j] + table[col_j][row_i]
            shear_sum = shear_sum + 0.5 * pair_sum * pair_sum
    return SMAGORINSKY * jnp.sqrt(shear_sum + STRAIN_FLOOR)


def tendency(interior, viscosity, table):
    centre_nu = viscosity[1:-1, :, 1:-1]
    centre_u = interior[:, 1:-1, :, 1:-1]

    def face_flux(nu_side, u_side):
        return 0.5 * (centre_nu + nu_side) * (u_side - centre_u)

    diffusion = face_flux(viscosity[2:, :, 1:-1], interior[:, 2:, :, 1:-1])
    diffusion = diffusion + face_flux(viscosity[:-2, :, 1:-1], interior[:, :-2, :, 1:-1])
    diffusion = diffusion + face_flux(roll_span(centre_nu, -1), roll_span(centre_u, -1))
    diffusion = diffusion + face_flux(roll_span(centre_nu, 1), roll_span(centre_u, 1))
    diffusion = diffusion + face_flux(viscosity[1:-1, :, 2:], interior[:, 1:-1, :, 2:])
    diffusion = diffusion + face_flux(viscosity[1:-1, :, :-2], interior[:, 1:-1, :, :-2])
    rows = []
    for comp in range(3):
        carried = (
            centre_u[0] * table[comp][0]
            + centre_u[1] * table[comp][1]
            + centre_u[2] * table[comp][2]
        )
        rows.append(carried)
    return diffusion - jnp.stack(rows)


def momentum(extended):
    padded = pad_depth(extended, 2)
    table = tensor_of(padded)
    viscosity = eddy_viscosity(table)
    centre_table = [[entry[1:-1, :, 1:-1] for entry in row] for row in table]
    return tendency(padded[:, 1:-1, :, 1:-1], viscosity, centre_table)


def corner_weights(cells, fractions, span_cells, depth_cells):
    plane_cells = span_cells * depth_cells
    lower_cell = jnp.maximum(cells, 0)
    stream_pos = lower_cell // plane_cells
    span_pos = lower_cell // depth_cells % span_cells
    depth_pos = lower_cell % depth_cells
    occupied = jnp.where(cells >= 0, 1.0, 0.0).astype(fractions.dtype)
    corner_list = []
    weight_list = []
    for shift_x in (0, 1):
        for shift_y in (0, 1):
            for shift_z in (0, 1):
                corner_list.append(
                    (stream_pos + shift_x) * plane_cells
                    + (span_pos + shift_y) % span_cells * depth_cells
                    + depth_pos
                    + shift_z
                )
                weight_x = fractions[0] if shift_x == 1 else 1.0 - fractions[0]
                weight_y = fractions[1] if shift_y == 1 else 1.0 - fractions[1]
                weight_z = fractions[2] if shift_z == 1 else 1.0 - fractions[2]
                weight_list.append(occupied * weight_x * weight_y * weight_z)
    return (jnp.stack(corner_list), jnp.stack(weight_list))


def blade_force(sampled, motion, direction, chord_row):
    relative = sampled - motion
    relative_speed = jnp.sqrt(jnp.sum(relative * relative, axis=0) + STRAIN_FLOOR)
    lift_dir = jnp.stack(
        [
            relative[1] * direction[2] - relative[2] * direction[1],
            relative[2] * direction[0] - relative[0] * direction[2],
            relative[0] * direction[1] - relative[1] * direction[0],
        ]
    )
    return FORCE_SCALE * chord_row * relative_speed * (lift_dir - relative)


def divergence(rim):
    padded = pad_depth(rim, 1)
    part_x = 0.5 * (padded[0, 2:, :, 1:-1] - padded[0, :-2, :, 1:-1])
    middle = padded[1, 1:-1, :, 1:-1]
    part_y = 0.5 * (roll_span(middle, -1) - roll_span(middle, 1))
    part_z = 0.5 * (padded[2, 1:-1, :, 2:] - padded[2, 1:-1, :, :-2])
    return part_x + part_y + part_z


def jacobi_step(potential_ext, source):
    padded = pad_depth(potential_ext, 1)
    centre = padded[1:-1, :, 1:-1]
    neighbour_sum = padded[2:, :, 1:-1] + padded[:-2, :, 1:-1]
    neighbour_sum = neighbour_sum + roll_span(centre, -1) + roll_span(centre, 1)
    neighbour_sum = neighbour_sum + padded[1:-1, :, 2:] + padded[1:-1, :, :-2]
    return (neighbour_sum - source) / 6.0


def correct(provisional, potential_ext):
    padded = pad_depth(potential_ext, 1)
    centre = padded[1:-1, :, 1:-1]
    grad_x = 0.5 * (padded[2:, :, 1:-1] - padded[:-2, :, 1:-1])
    grad_y = 0.5 * (roll_span(centre, -1) - roll_span(centre, 1))
    grad_z = 0.5 * (padded[1:-1, :, 2:] - padded[1:-1, :, :-2])
    return provisional - jnp.stack([grad_x, grad_y, grad_z])


def potential_rim(potential):
    return padded_2(potential, (("gx", 0),), 1)


def shards(velocity, inflow, blade_motion, blade_axis, blade_chord, host_cell, host_frac):
    tile_index = lax.axis_index("gx")
    stream_cells = velocity.shape[1]
    span_cells = velocity.shape[2]
    depth_cells = velocity.shape[3]
    inlet = lax.all_gather(inflow, "gx", axis=1, tiled=True)
    widened = padded_2(velocity, (("gx", 1),), 2)
    lower = jnp.where(tile_index == 0, jnp.stack([inlet, inlet], axis=1), widened[:, :2])
    tendency_here = momentum(jnp.concatenate([lower, widened[:, 2:]], axis=1))
    corners, weights = corner_weights(host_cell, host_frac, span_cells, depth_cells)
    flat_velocity = velocity.reshape(3, stream_cells * span_cells * depth_cells)
    sampled = jnp.sum(weights[None] * flat_velocity[:, corners], axis=1)
    arrived = lax.all_to_all(sampled, "gx", split_axis=1, concat_axis=1, tiled=True)
    own_force = blade_force(arrived, blade_motion, blade_axis, blade_chord)
    slot_force = lax.all_to_all(own_force, "gx", split_axis=1, concat_axis=1, tiled=True)
    spread = (
        jnp.zeros((3, stream_cells * span_cells * depth_cells), jnp.float32)
        .at[:, corners.reshape(-1)]
        .add((slot_force[:, None, :] * weights[None]).reshape(3, -1))
    )
    provisional = velocity + TIME_STEP * (tendency_here + spread.reshape(velocity.shape))
    rim = padded_2(provisional, (("gx", 1),), 1)
    source = divergence(rim)
    potential = -source / 6.0
    for sweep_no in range(JACOBI - 1):
        potential = jacobi_step(potential_rim(potential), source)
    final_ext = potential_rim(potential)
    return correct(provisional, final_ext)


def solution(mesh):
    return jax.shard_map(
        shards,
        mesh=mesh,
        in_specs=(
            P("runs", "gx", None, None),
            P("runs", "gx", None),
            P("runs", "gx"),
            P("runs", "gx"),
            P(("runs", "gx")),
            P(("runs", "gx")),
            P("runs", "gx"),
        ),
        out_specs=P("runs", "gx", None, None),
        check_vma=False,
    )
```

profile of v0, /device:TPU:8, one launch (start us, length us, event | category | flops | bytes accessed | tf_op | source)
XLA Modules:
  0.0 170.4 jit_solution(14183589694891313093)
XLA Ops:
  1.4 0.8 fusion.108
  2.2 17.7 %copy.23 = f32[3,4,128,128]{0,3,2,1:T(8,128)} copy(f32[3,4,128,128]{3,2,1,0:T(8,128)} %param.7) | data formatting | bytes 1572864 | tf_op args[0]
  20.1 13.1 %gather_fusion = f32[1536,3]{1,0:T(8,128)S(1)} fusion(f32[3,65536]{0,1:T(8,128)} %bitcast.124, s32[2048]{0:T(1024)S(1)} %pad_clamp_fusion), kind=kCustom, calls=%fused_computation | custom fusion | bytes 43008 | tf_op jit(solution)/shard_map/gather | solution.py:166
  34.4 6.3 %all-to-all-start = ((f32[3,16,12]{2,0,1:T(4,128)}), f32[3,16,12]{2,0,1:T(4,128)S(1)}, u32[]{:S(2)}, u32[]{:S(2)}) async-start(f32[3,16,12]{2,0,1:T(4,128)} %copy.25), calls=%async_computation | async-start | bytes 65536 | tf_op jit(solution)/shard_map/all_to_all | solution.py:167
  40.7 0.9 fusion.98
  41.7 3.1 %collective-permute-start.1 = (f32[3,2,128,128]{3,2,1,0:T(8,128)}, f32[3,2,128,128]{3,2,1,0:T(8,128)S(1)}, u32[]{:S(2)}, u32[]{:S(2)}) collective-permute-start(f32[3,2,128,128]{3,2,1,0:T(8,128)} %get-tuple-element.57), channel_id=1, source_target_pairs={{1,0},{2,1},{3,2},{4,3},{5,4},{6,5},{7,6},{8,7},{9,8},{10,9},{11,1... | collective-permute-start | bytes 1179656 | tf_op jit(solution)/shard_map/ppermute | solution.py:23
  44.8 1.9 %collective-permute-start = (f32[3,2,128,128]{3,2,1,0:T(8,128)}, f32[3,2,128,128]{3,2,1,0:T(8,128)}, u32[]{:S(2)}, u32[]{:S(2)}) collective-permute-start(f32[3,2,128,128]{3,2,1,0:T(8,128)} %get-tuple-element.56), channel_id=1, source_target_pairs={{0,1},{1,2},{2,3},{3,4},{4,5},{5,6},{6,7},{7,8},{8,9},{9,10},{10,1... | collective-permute-start | bytes 1179656 | tf_op jit(solution)/shard_map/ppermute | solution.py:22
  49.1 6.3 %all-to-all-start.1 = ((f32[3,16,12]{2,0,1:T(4,128)}), f32[3,16,12]{2,0,1:T(4,128)S(1)}, u32[]{:S(2)}, u32[]{:S(2)}) async-start(f32[3,16,12]{2,0,1:T(4,128)} %copy.27), calls=%async_computation.1 | async-start | bytes 65536 | tf_op jit(solution)/shard_map/all_to_all | solution.py:169
  55.4 20.5 %all_gather.3 = f32[3,128,128]{2,1,0:T(8,128)} all-gather(f32[3,8,128]{2,1,0:T(8,128)S(1)} %copy-done.2), channel_id=1, replica_groups=mesh['runs'=2,'gx'=16] {'gx'}, dimensions={1}, use_global_device_ids=true | all-gather | bytes 208896 | tf_op jit(solution)/shard_map/all_gather | solution.py:160
  76.8 1.2 bitcast_multiply_fusion
  78.0 24.5 %scatter_custom_fusion = f32[3,65536]{0,1:T(8,128)} fusion(s32[1536]{0:T(1024)} %fusion.75, f32[]{:T(128)} %constant.100.clone.1, f32[3,1536]{0,1:T(8,128)S(1)} %bitcast_multiply_fusion), kind=kCustom, calls=%fused_computation.2 | custom fusion | flops 4608 | bytes 805376 | tf_op jit(solution)/shard_map/scatter-add | solution.py:173
  102.5 19.5 %copy.30 = f32[3,4,128,128]{3,2,1,0:T(8,128)S(1)} copy(f32[3,4,128,128]{0,3,2,1:T(8,128)} %bitcast.123) | data formatting | bytes 1572864 | tf_op jit(solution)/shard_map/reshape | solution.py:175
  122.0 1.2 maximum_select_fusion
  123.2 0.9 select_maximum_fusion
  124.0 1.9 %fusion.4 = (f32[3,6,128,130]{3,2,1,0:T(8,128)S(1)}, f32[3,6,128,130]{3,2,1,0:T(8,128)S(1)}) fusion(f32[3,8,128,132]{3,2,1,0:T(8,128)S(1)} %select_maximum_fusion), kind=kLoop, calls=%fused_computation.16 | loop fusion | flops 1198080 | bytes 7188480 | tf_op jit(solution)/shard_map/mul | solution.py:38
  126.1 1.3 fusion.92
  128.3 0.9 fusion.17
  130.6 0.8 fusion.23
  131.5 2.4 %collective-permute-start.2 = (f32[3,1,128,128]{3,2,1,0:T(8,128)S(1)}, f32[3,1,128,128]{3,2,1,0:T(8,128)S(1)}, u32[]{:S(2)}, u32[]{:S(2)}) collective-permute-start(f32[3,1,128,128]{3,2,1,0:T(8,128)S(1)} %get-tuple-element.38), channel_id=1, source_target_pairs={{1,0},{2,1},{3,2},{4,3},{5,4},{6,5},{7,6},{8,7},{9,8},{10,9},{11,1... | collective-permute-start | bytes 589832 | tf_op jit(solution)/shard_map/ppermute | solution.py:23
  133.9 1.9 %collective-permute-start.3 = (f32[3,1,128,128]{3,2,1,0:T(8,128)S(1)}, f32[3,1,128,128]{3,2,1,0:T(8,128)S(1)}, u32[]{:S(2)}, u32[]{:S(2)}) collective-permute-start(f32[3,1,128,128]{3,2,1,0:T(8,128)S(1)} %get-tuple-element.37), channel_id=1, source_target_pairs={{0,1},{1,2},{2,3},{3,4},{4,5},{5,6},{6,7},{7,8},{8,9},{9,10},{10,1... | collective-permute-start | bytes 589832 | tf_op jit(solution)/shard_map/ppermute | solution.py:22
  135.9 1.2 collective-permute-done.2
  137.0 4.7 %collective-permute-done.3 = f32[3,1,128,128]{3,2,1,0:T(8,128)S(1)} collective-permute-done((f32[3,1,128,128]{3,2,1,0:T(8,128)S(1)}, f32[3,1,128,128]{3,2,1,0:T(8,128)S(1)}, u32[]{:S(2)}, u32[]{:S(2)}) %collective-permute-start.3) | collective-permute-done | bytes 196640 | tf_op jit(solution)/shard_map/ppermute | solution.py:22
  142.7 1.9 %collective-permute-start.4 = (f32[1,128,128]{2,1,0:T(8,128)S(1)}, f32[1,128,128]{2,1,0:T(8,128)S(1)}, u32[]{:S(2)}, u32[]{:S(2)}) collective-permute-start(f32[1,128,128]{2,1,0:T(8,128)S(1)} %get-tuple-element.75), channel_id=1, source_target_pairs={{1,0},{2,1},{3,2},{4,3},{5,4},{6,5},{7,6},{8,7},{9,8},{10,9},{11,1... | collective-permute-start | bytes 196616 | tf_op jit(solution)/shard_map/ppermute | solution.py:23
  144.6 2.4 %collective-permute-start.5 = (f32[1,128,128]{2,1,0:T(8,128)S(1)}, f32[1,128,128]{2,1,0:T(8,128)S(1)}, u32[]{:S(2)}, u32[]{:S(2)}) collective-permute-start(f32[1,128,128]{2,1,0:T(8,128)S(1)} %get-tuple-element.74), channel_id=1, source_target_pairs={{0,1},{1,2},{2,3},{3,4},{4,5},{5,6},{6,7},{7,8},{8,9},{9,10},{10,1... | collective-permute-start | bytes 196616 | tf_op jit(solution)/shard_map/ppermute | solution.py:22
  147.1 4.0 %collective-permute-done.5 = f32[1,128,128]{2,1,0:T(8,128)S(1)} collective-permute-done((f32[1,128,128]{2,1,0:T(8,128)S(1)}, f32[1,128,128]{2,1,0:T(8,128)S(1)}, u32[]{:S(2)}, u32[]{:S(2)}) %collective-permute-start.5) | collective-permute-done | bytes 65568 | tf_op jit(solution)/shard_map/ppermute | solution.py:22
  151.6 1.9 %collective-permute-start.6 = (f32[1,128,128]{2,1,0:T(8,128)S(1)}, f32[1,128,128]{2,1,0:T(8,128)S(1)}, u32[]{:S(2)}, u32[]{:S(2)}) collective-permute-start(f32[1,128,128]{2,1,0:T(8,128)S(1)} %get-tuple-element.69), channel_id=1, source_target_pairs={{1,0},{2,1},{3,2},{4,3},{5,4},{6,5},{7,6},{8,7},{9,8},{10,9},{11,1... | collective-permute-start | bytes 196616 | tf_op jit(solution)/shard_map/ppermute | solution.py:23
  153.5 2.4 %collective-permute-start.7 = (f32[1,128,128]{2,1,0:T(8,128)S(1)}, f32[1,128,128]{2,1,0:T(8,128)S(1)}, u32[]{:S(2)}, u32[]{:S(2)}) collective-permute-start(f32[1,128,128]{2,1,0:T(8,128)S(1)} %get-tuple-element.68), channel_id=1, source_target_pairs={{0,1},{1,2},{2,3},{3,4},{4,5},{5,6},{6,7},{7,8},{8,9},{9,10},{10,1... | collective-permute-start | bytes 196616 | tf_op jit(solution)/shard_map/ppermute | solution.py:22
  156.0 4.0 %collective-permute-done.7 = f32[1,128,128]{2,1,0:T(8,128)S(1)} collective-permute-done((f32[1,128,128]{2,1,0:T(8,128)S(1)}, f32[1,128,128]{2,1,0:T(8,128)S(1)}, u32[]{:S(2)}, u32[]{:S(2)}) %collective-permute-start.7) | collective-permute-done | bytes 65568 | tf_op jit(solution)/shard_map/ppermute | solution.py:22
  160.5 1.9 %collective-permute-start.8 = (f32[1,128,128]{2,1,0:T(8,128)S(1)}, f32[1,128,128]{2,1,0:T(8,128)S(1)}, u32[]{:S(2)}, u32[]{:S(2)}) collective-permute-start(f32[1,128,128]{2,1,0:T(8,128)S(1)} %get-tuple-element.63), channel_id=1, source_target_pairs={{1,0},{2,1},{3,2},{4,3},{5,4},{6,5},{7,6},{8,7},{9,8},{10,9},{11,1... | collective-permute-start | bytes 196616 | tf_op jit(solution)/shard_map/ppermute | solution.py:23
  162.5 2.4 %collective-permute-start.9 = (f32[1,128,128]{2,1,0:T(8,128)S(1)}, f32[1,128,128]{2,1,0:T(8,128)S(1)}, u32[]{:S(2)}, u32[]{:S(2)}) collective-permute-start(f32[1,128,128]{2,1,0:T(8,128)S(1)} %get-tuple-element.62), channel_id=1, source_target_pairs={{0,1},{1,2},{2,3},{3,4},{4,5},{5,6},{6,7},{7,8},{8,9},{9,10},{10,1... | collective-permute-start | bytes 196616 | tf_op jit(solution)/shard_map/ppermute | solution.py:22
  164.9 4.0 %collective-permute-done.9 = f32[1,128,128]{2,1,0:T(8,128)S(1)} collective-permute-done((f32[1,128,128]{2,1,0:T(8,128)S(1)}, f32[1,128,128]{2,1,0:T(8,128)S(1)}, u32[]{:S(2)}, u32[]{:S(2)}) %collective-permute-start.9) | collective-permute-done | bytes 65568 | tf_op jit(solution)/shard_map/ppermute | solution.py:22
  169.4 1.0 maximum_subtract_fusion.3
  (89 shorter events, 10.8 us)
Async XLA Ops:
  2.2 17.9 %copy-start.3 = (s32[192]{0:T(256)S(1)}, s32[192]{0:T(256)}, u32[]{:S(2)}) copy-start(s32[192]{0:T(256)} %param.12) | copy-start | bytes 2308
  2.2 38.5 %copy-start = (f32[3,4,128,128]{3,2,1,0:T(8,128)S(1)}, f32[3,4,128,128]{3,2,1,0:T(8,128)}, u32[]{:S(2)}) copy-start(f32[3,4,128,128]{3,2,1,0:T(8,128)} %param.7) | copy-start | bytes 2359300
  34.4 13.8 %all-to-all-start = ((f32[3,16,12]{2,0,1:T(4,128)}), f32[3,16,12]{2,0,1:T(4,128)S(1)}, u32[]{:S(2)}, u32[]{:S(2)}) async-start(f32[3,16,12]{2,0,1:T(4,128)} %copy.25), calls=%async_computation | async-start | bytes 65536 | tf_op jit(solution)/shard_map/all_to_all | solution.py:167
  40.7 7.6 %copy-start.4 = (f32[3,192]{1,0:T(4,128)S(1)}, f32[3,192]{1,0:T(4,128)}, u32[]{:S(2)}) copy-start(f32[3,192]{1,0:T(4,128)} %param.9) | copy-start | bytes 6916
  40.7 7.6 %copy-start.5 = (f32[3,192]{1,0:T(4,128)S(1)}, f32[3,192]{1,0:T(4,128)}, u32[]{:S(2)}) copy-start(f32[3,192]{1,0:T(4,128)} %param.10) | copy-start | bytes 6916
  40.7 7.7 %copy-start.6 = (f32[192]{0:T(256)S(1)}, f32[192]{0:T(256)}, u32[]{:S(2)}) copy-start(f32[192]{0:T(256)} %param.11) | copy-start | bytes 2308
  40.7 14.7 %copy-start.2 = (f32[3,8,128]{2,1,0:T(8,128)S(1)}, f32[3,8,128]{2,1,0:T(8,128)}, u32[]{:S(2)}) copy-start(f32[3,8,128]{2,1,0:T(8,128)} %param.8) | copy-start | bytes 36868
  41.7 81.5 %collective-permute-start.1 = (f32[3,2,128,128]{3,2,1,0:T(8,128)}, f32[3,2,128,128]{3,2,1,0:T(8,128)S(1)}, u32[]{:S(2)}, u32[]{:S(2)}) collective-permute-start(f32[3,2,128,128]{3,2,1,0:T(8,128)} %get-tuple-element.57), channel_id=1, source_target_pairs={{1,0},{2,1},{3,2},{4,3},{5,4},{6,5},{7,6},{8,7},{9,8},{10,9},{11,1... | collective-permute-start | bytes 1179656 | tf_op jit(solution)/shard_map/ppermute | solution.py:23
  44.8 77.2 %collective-permute-start = (f32[3,2,128,128]{3,2,1,0:T(8,128)}, f32[3,2,128,128]{3,2,1,0:T(8,128)}, u32[]{:S(2)}, u32[]{:S(2)}) collective-permute-start(f32[3,2,128,128]{3,2,1,0:T(8,128)} %get-tuple-element.56), channel_id=1, source_target_pairs={{0,1},{1,2},{2,3},{3,4},{4,5},{5,6},{6,7},{7,8},{8,9},{9,10},{10,1... | collective-permute-start | bytes 1179656 | tf_op jit(solution)/shard_map/ppermute | solution.py:22
  49.1 26.9 %all-to-all-start.1 = ((f32[3,16,12]{2,0,1:T(4,128)}), f32[3,16,12]{2,0,1:T(4,128)S(1)}, u32[]{:S(2)}, u32[]{:S(2)}) async-start(f32[3,16,12]{2,0,1:T(4,128)} %copy.27), calls=%async_computation.1 | async-start | bytes 65536 | tf_op jit(solution)/shard_map/all_to_all | solution.py:169
  129.8 0.7 copy-start.1
  131.5 5.6 %collective-permute-start.2 = (f32[3,1,128,128]{3,2,1,0:T(8,128)S(1)}, f32[3,1,128,128]{3,2,1,0:T(8,128)S(1)}, u32[]{:S(2)}, u32[]{:S(2)}) collective-permute-start(f32[3,1,128,128]{3,2,1,0:T(8,128)S(1)} %get-tuple-element.38), channel_id=1, source_target_pairs={{1,0},{2,1},{3,2},{4,3},{5,4},{6,5},{7,6},{8,7},{9,8},{10,9},{11,1... | collective-permute-start | bytes 589832 | tf_op jit(solution)/shard_map/ppermute | solution.py:23
  133.9 7.9 %collective-permute-start.3 = (f32[3,1,128,128]{3,2,1,0:T(8,128)S(1)}, f32[3,1,128,128]{3,2,1,0:T(8,128)S(1)}, u32[]{:S(2)}, u32[]{:S(2)}) collective-permute-start(f32[3,1,128,128]{3,2,1,0:T(8,128)S(1)} %get-tuple-element.37), channel_id=1, source_target_pairs={{0,1},{1,2},{2,3},{3,4},{4,5},{5,6},{6,7},{7,8},{8,9},{9,10},{10,1... | collective-permute-start | bytes 589832 | tf_op jit(solution)/shard_map/ppermute | solution.py:22
  142.7 4.4 %collective-permute-start.4 = (f32[1,128,128]{2,1,0:T(8,128)S(1)}, f32[1,128,128]{2,1,0:T(8,128)S(1)}, u32[]{:S(2)}, u32[]{:S(2)}) collective-permute-start(f32[1,128,128]{2,1,0:T(8,128)S(1)} %get-tuple-element.75), channel_id=1, source_target_pairs={{1,0},{2,1},{3,2},{4,3},{5,4},{6,5},{7,6},{8,7},{9,8},{10,9},{11,1... | collective-permute-start | bytes 196616 | tf_op jit(solution)/shard_map/ppermute | solution.py:23
  144.6 6.5 %collective-permute-start.5 = (f32[1,128,128]{2,1,0:T(8,128)S(1)}, f32[1,128,128]{2,1,0:T(8,128)S(1)}, u32[]{:S(2)}, u32[]{:S(2)}) collective-permute-start(f32[1,128,128]{2,1,0:T(8,128)S(1)} %get-tuple-element.74), channel_id=1, source_target_pairs={{0,1},{1,2},{2,3},{3,4},{4,5},{5,6},{6,7},{7,8},{8,9},{9,10},{10,1... | collective-permute-start | bytes 196616 | tf_op jit(solution)/shard_map/ppermute | solution.py:22
  151.6 4.4 %collective-permute-start.6 = (f32[1,128,128]{2,1,0:T(8,128)S(1)}, f32[1,128,128]{2,1,0:T(8,128)S(1)}, u32[]{:S(2)}, u32[]{:S(2)}) collective-permute-start(f32[1,128,128]{2,1,0:T(8,128)S(1)} %get-tuple-element.69), channel_id=1, source_target_pairs={{1,0},{2,1},{3,2},{4,3},{5,4},{6,5},{7,6},{8,7},{9,8},{10,9},{11,1... | collective-permute-start | bytes 196616 | tf_op jit(solution)/shard_map/ppermute | solution.py:23
  153.5 6.5 %collective-permute-start.7 = (f32[1,128,128]{2,1,0:T(8,128)S(1)}, f32[1,128,128]{2,1,0:T(8,128)S(1)}, u32[]{:S(2)}, u32[]{:S(2)}) collective-permute-start(f32[1,128,128]{2,1,0:T(8,128)S(1)} %get-tuple-element.68), channel_id=1, source_target_pairs={{0,1},{1,2},{2,3},{3,4},{4,5},{5,6},{6,7},{7,8},{8,9},{9,10},{10,1... | collective-permute-start | bytes 196616 | tf_op jit(solution)/shard_map/ppermute | solution.py:22
  160.5 4.4 %collective-permute-start.8 = (f32[1,128,128]{2,1,0:T(8,128)S(1)}, f32[1,128,128]{2,1,0:T(8,128)S(1)}, u32[]{:S(2)}, u32[]{:S(2)}) collective-permute-start(f32[1,128,128]{2,1,0:T(8,128)S(1)} %get-tuple-element.63), channel_id=1, source_target_pairs={{1,0},{2,1},{3,2},{4,3},{5,4},{6,5},{7,6},{8,7},{9,8},{10,9},{11,1... | collective-permute-start | bytes 196616 | tf_op jit(solution)/shard_map/ppermute | solution.py:23
  162.5 6.5 %collective-permute-start.9 = (f32[1,128,128]{2,1,0:T(8,128)S(1)}, f32[1,128,128]{2,1,0:T(8,128)S(1)}, u32[]{:S(2)}, u32[]{:S(2)}) collective-permute-start(f32[1,128,128]{2,1,0:T(8,128)S(1)} %get-tuple-element.62), channel_id=1, source_target_pairs={{0,1},{1,2},{2,3},{3,4},{4,5},{5,6},{6,7},{7,8},{8,9},{9,10},{10,1... | collective-permute-start | bytes 196616 | tf_op jit(solution)/shard_map/ppermute | solution.py:22
where the time goes:
time: 172 us; the launch traced here: 170 us
  local copies, waits for them, and re-layouts  58 us (34%)
  other arithmetic  38.4 us (22%)
  starting transfers between devices  34.9 us (20%)
  blocking collectives  20.5 us (12%)
  waiting for transfers between devices  18 us (10%)
    scatter-add x1, other arithmetic, shards(): spread = jnp.zeros((3, stream_cells * span_cells * depth_cells), jnp.floa...  24.5 us
    all_gather x1, blocking collectives, shards(): inlet = lax.all_gather(inflow, 'gx', axis=1, tiled=True)  20.5 us
    reshape x1, local copies, waits for them, and re-layouts, shards(): spread.reshape(velocity.shape)  19.5 us
    unnamed x22, local copies, waits for them, and re-layouts  17.8 us
    ppermute x5, waiting for transfers between devices, padded_2(): before = lax.ppermute(last, axis, up)  16.8 us
    gather x1, local copies, waits for them, and re-layouts, shards(): sampled = jnp.sum(weights[None] * flat_velocity[:, corners], axis=1)  13.1 us
    ppermute x5, starting transfers between devices, padded_2(): after = lax.ppermute(initial, axis, down)  11.3 us
    ppermute x5, starting transfers between devices, padded_2(): before = lax.ppermute(last, axis, up)  11.1 us
  transfers between devices with their start and end apart: 12, of which 5 were waited for; matrix products, arithmetic and copies ran while one was open for 30% of the time, Pallas kernels for 0%

commit v1 on v0

v1 whole, which is shorter than its diff:
```python
import functools

import jax
import jax.numpy as jnp
from jax import lax
from jax.experimental import pallas as pl
from jax.experimental.pallas import tpu as pltpu
from jax.sharding import PartitionSpec as P

TIME_STEP = 0.2
SMAGORINSKY = 0.0289
STRAIN_FLOOR = 0.01
FORCE_SCALE = 0.2

MESH = pl.DeviceIdType.MESH
PAD = 8
ROWS = 16
SLOT = 16
LANES = 128


def split(value):
    high = value.astype(jnp.bfloat16)
    return high, (value - high.astype(jnp.float32)).astype(jnp.bfloat16)


def product(left, right, contract):
    def one(a, b):
        return lax.dot_general(
            a, b, (contract, ((), ())), preferred_element_type=jnp.float32
        )

    return one(left[0], right[0]) + (one(left[0], right[1]) + one(left[1], right[0]))


def kernel(
    n,
    vel,
    inflow,
    motion,
    axis,
    chord,
    cell,
    frac,
    out,
    u,
    nu,
    prov,
    p1,
    p2,
    p3,
    part_out,
    part_in,
    rows,
    blocks,
    table,
    arrived,
    inlet,
    load_sem,
    halo_send,
    halo_recv,
    blade_send,
    blade_recv,
    in_send,
    in_recv,
    rim_send,
    rim_recv,
):
    me = lax.axis_index("gx")
    cx, ny, nz = vel.shape[1:]
    cap = cell.shape[1] // n
    body = pl.ds(PAD, ny)
    has_low, has_high = me > 0, me < n - 1
    low_ok = jnp.where(has_low, 1.0, 0.0)
    high_ok = jnp.where(has_high, 1.0, 0.0)

    barrier = pltpu.get_barrier_semaphore()

    def greet(k, carry):
        pl.semaphore_signal(
            barrier, inc=1, device_id={"gx": lax.rem(me + k, n)}, device_id_type=MESH
        )
        return carry

    lax.fori_loop(1, n, greet, 0)
    load = pltpu.make_async_copy(vel, u.at[:, 2 : 2 + cx, body], load_sem)
    load.start()

    zeros = jnp.zeros((16, rows.shape[1]), jnp.float32)
    rows[...] = zeros
    rows[0:3] = motion[...]
    rows[3:6] = axis[...]
    rows[6:7] = chord[...]
    rows[8:9] = (cell[...] + 1).astype(jnp.float32)
    rows[9:12] = frac[...]
    owners = 256 // SLOT
    wide = owners * cap
    source_lane = lax.broadcasted_iota(jnp.int32, (wide, 256), 0)
    slot_lane = lax.broadcasted_iota(jnp.int32, (wide, 256), 1)
    within = slot_lane & (SLOT - 1)
    picked = (source_lane == (slot_lane >> 4) * cap + within) & (within < cap)
    pick = jnp.where(picked, 1.0, 0.0)
    chunks = n // owners
    for q in range(chunks):
        spaced = lax.dot_general(
            rows[:, q * wide : (q + 1) * wide],
            pick,
            (((1,), (0,)), ((), ())),
            precision=lax.Precision.HIGHEST,
            preferred_element_type=jnp.float32,
        )
        table[q] = spaced[8:16]
        for h in range(256 // LANES):
            blocks[q * (256 // LANES) + h] = spaced[0:8, h * LANES : (h + 1) * LANES]

    def halo(up):
        if up:
            src, dst, to = vel.at[:, cx - 2 : cx], u.at[:, 0:2, body], me + 1
        else:
            src, dst, to = vel.at[:, 0:2], u.at[:, cx + 2 : cx + 4, body], me - 1
        return pltpu.make_async_remote_copy(
            src_ref=src,
            dst_ref=dst,
            send_sem=halo_send.at[int(up)],
            recv_sem=halo_recv.at[int(up)],
            device_id={"gx": to},
            device_id_type=MESH,
        )

    per = LANES // SLOT

    def blade(k, to, slot):
        return pltpu.make_async_remote_copy(
            src_ref=blocks.at[to // per],
            dst_ref=arrived.at[slot],
            send_sem=blade_send.at[k],
            recv_sem=blade_recv.at[k],
            device_id={"gx": to},
            device_id_type=MESH,
        )

    def feed(slot):
        return pltpu.make_async_remote_copy(
            src_ref=inflow,
            dst_ref=inlet.at[slot],
            send_sem=in_send,
            recv_sem=in_recv.at[slot],
            device_id={"gx": 0},
            device_id_type=MESH,
        )

    pl.semaphore_wait(barrier, n - 1)

    @pl.when(has_low)
    def _():
        feed(me).start()
        halo(False).start()

    @pl.when(has_high)
    def _():
        halo(True).start()

    def send_blade(k, carry):
        blade(k, lax.rem(me + k, n), me).start()
        return carry

    lax.fori_loop(1, n, send_blade, 0)
    arrived[me] = blocks[me // per]

    @pl.when(jnp.logical_not(has_high))
    def _():
        u[:, cx + 2 : cx + 4] = jnp.zeros((3, 2) + u.shape[2:], jnp.float32)
        prov[0, cx + 1] = jnp.zeros(prov.shape[2:], jnp.float32)
        p1[cx + 4 : cx + 6] = jnp.zeros((2,) + p1.shape[1:], jnp.float32)
        part_in[1] = jnp.zeros(part_in.shape[1:], jnp.float32)

    @pl.when(jnp.logical_not(has_low))
    def _():
        prov[0, 0] = jnp.zeros(prov.shape[2:], jnp.float32)
        p1[0:2] = jnp.zeros((2,) + p1.shape[1:], jnp.float32)
        part_in[0] = jnp.zeros(part_in.shape[1:], jnp.float32)

    def wrap(ref, *lead):
        ref[(*lead, slice(PAD - 1, PAD))] = ref[(*lead, slice(PAD + ny - 1, PAD + ny))]
        ref[(*lead, slice(PAD + ny, PAD + ny + 1))] = ref[(*lead, slice(PAD, PAD + 1))]

    load.wait()
    for i in range(3):
        for x in range(cx):
            wrap(u, i, x + 2)

    depth_bits, span_bits = nz.bit_length() - 1, ny.bit_length() - 1
    layer = lax.broadcasted_iota(jnp.int32, (LANES, 256), 0)

    def weights(q):
        info = table[q]
        where = (info[0:1] + 0.5).astype(jnp.int32) - 1
        full = where >= 0
        a = where >> (depth_bits + span_bits)
        b = (where >> depth_bits) & (ny - 1)
        d = where & (nz - 1)
        fx, fy, fz = info[1:2], info[2:3], info[3:4]
        along_z = jnp.where(layer == d, 1.0 - fz, jnp.where(layer == d + 1, fz, 0.0))
        next_b = (b + 1) & (ny - 1)
        along_y = jnp.where(layer == b, 1.0 - fy, jnp.where(layer == next_b, fy, 0.0))
        along_x = []
        for x in range(cx):
            kept = jnp.where(a == x, 1.0 - fx, jnp.where(a + 1 == x, fx, 0.0))
            along_x.append(jnp.where(full, kept, 0.0))
        return along_x, along_y, split(along_z)

    sampled = []
    for q in range(chunks):
        along_x, along_y, along_z = weights(q)
        for i in range(3):
            total = jnp.zeros((1, 256), jnp.float32)
            for x in range(cx):
                lines = product(split(u[i, x + 2, body]), along_z, ((1,), (0,)))
                total = total + along_x[x] * jnp.sum(lines * along_y, axis=0, keepdims=True)
            sampled.append(total)

    def take_blade(k, carry):
        blade(k, me, lax.rem(me + n - k, n)).wait_recv()
        return carry

    lax.fori_loop(1, n, take_blade, 0)
    lane = lax.broadcasted_iota(jnp.int32, (8, LANES), 1)
    mine = lax.rem(me, per)
    for q in range(chunks):
        halves = []
        for h in range(256 // LANES):
            block = jnp.zeros((8, LANES), jnp.float32)
            for o in range(per):
                shift = lax.rem(o - mine + per, per) * SLOT
                moved = pltpu.roll(arrived[(q * (256 // LANES) + h) * per + o], shift, 1)
                block = jnp.where((lane >> 4) == o, moved, block)
            halves.append(block)
        point = jnp.concatenate(halves, axis=1)
        along_x, along_y, along_z = weights(q)
        r = [sampled[3 * q + i] - point[i : i + 1] for i in range(3)]
        e = [point[3 + i : 4 + i] for i in range(3)]
        speed = jnp.sqrt(r[0] * r[0] + r[1] * r[1] + r[2] * r[2] + STRAIN_FLOOR)
        size = (TIME_STEP * FORCE_SCALE) * point[6:7] * speed
        lift = [
            r[1] * e[2] - r[2] * e[1],
            r[2] * e[0] - r[0] * e[2],
            r[0] * e[1] - r[1] * e[0],
        ]
        for i in range(3):
            force = size * (lift[i] - r[i])
            for x in range(cx):
                laid = product(
                    split(along_y * (force * along_x[x])), along_z, ((1,), (1,))
                )
                if q == 0:
                    prov[i, x + 1, body] = laid
                else:
                    prov[i, x + 1, body] += laid

    @pl.when(has_low)
    def _():
        halo(True).wait_recv()

    @pl.when(has_high)
    def _():
        halo(False).wait_recv()

    @pl.when(jnp.logical_not(has_low))
    def _():
        def take_inlet(k, carry):
            feed(k).wait_recv()
            return carry

        lax.fori_loop(1, n, take_inlet, 0)
        inlet[0] = inflow[...]
        share = inflow.shape[1]
        for k in range(n):
            at = slice(PAD + k * share, PAD + (k + 1) * share)
            for i in range(3):
                u[i, 0, at] = inlet[k, i]
                u[i, 1, at] = inlet[k, i]

    for i in range(3):
        wrap(u, i, 1)
        wrap(u, i, cx + 2)

    first = lax.broadcasted_iota(jnp.int32, (ROWS, nz), 1) == 0
    last = lax.broadcasted_iota(jnp.int32, (ROWS, nz), 1) == nz - 1

    def deeper(value, edge=0.0):
        return jnp.where(last, edge, pltpu.roll(value, nz - 1, 1))

    def shallower(value, edge=0.0):
        return jnp.where(first, edge, pltpu.roll(value, 1, 1))

    starts = range(PAD, PAD + ny, ROWS)

    def at(start, shift=0):
        return pl.ds(start + shift, ROWS)

    def viscosity(p, carry):
        for s in starts:
            d = []
            for i in range(3):
                centre = u[i, p + 1, at(s)]
                d.append(
                    (
                        u[i, p + 2, at(s)] - u[i, p, at(s)],
                        u[i, p + 1, at(s, 1)] - u[i, p + 1, at(s, -1)],
                        deeper(centre) - shallower(centre),
                    )
                )
            xy, xz, yz = d[0][1] + d[1][0], d[0][2] + d[2][0], d[1][2] + d[2][1]
            shear = d[0][0] * d[0][0] + d[1][1] * d[1][1] + d[2][2] * d[2][2]
            shear = shear + shear + (xy * xy + xz * xz + yz * yz) + 4.0 * STRAIN_FLOOR
            nu[p, at(s)] = (0.25 * TIME_STEP * SMAGORINSKY) * jnp.sqrt(shear)
        wrap(nu, p)
        return carry

    lax.fori_loop(0, cx + 2, viscosity, 0)

    def momentum(p, carry):
        for s in starts:
            centre = [u[i, p + 2, at(s)] for i in range(3)]
            own = nu[p + 1, at(s)]
            edge = centre[2] * centre[2]
            edge = edge + edge + centre[0] * centre[0] + centre[1] * centre[1]
            edge = (0.25 * TIME_STEP * SMAGORINSKY) * jnp.sqrt(edge + 4.0 * STRAIN_FLOOR)
            carried = [(0.5 * TIME_STEP) * value for value in centre]
            coef = [
                own + nu[p + 2, at(s)] - carried[0],
                own + nu[p, at(s)] + carried[0],
                own + nu[p + 1, at(s, 1)] - carried[1],
                own + nu[p + 1, at(s, -1)] + carried[1],
                own + deeper(own, edge) - carried[2],
                own + shallower(own, edge) + carried[2],
            ]
            rest = 1.0 - (coef[0] + coef[1] + coef[2] + coef[3] + coef[4] + coef[5])
            for i in range(3):
                value = prov[i, p + 1, at(s)] + rest * centre[i]
                value = value + coef[0] * u[i, p + 3, at(s)] + coef[1] * u[i, p + 1, at(s)]
                value = value + coef[2] * u[i, p + 2, at(s, 1)] + coef[3] * u[i, p + 2, at(s, -1)]
                value = value + coef[4] * deeper(centre[i]) + coef[5] * shallower(centre[i])
                prov[i, p + 1, at(s)] = value
        wrap(prov, 1, p + 1)
        return carry

    lax.fori_loop(0, cx, momentum, 0)

    scale = -1.0 / 12.0

    def flat_part(p, s):
        w = prov[2, p + 1, at(s)]
        return prov[1, p + 1, at(s, 1)] - prov[1, p + 1, at(s, -1)] + deeper(w) - shallower(w)

    def rim(up, what):
        if what == 0:
            src = prov.at[0, cx if up else 1, body]
            dst = prov.at[0, 0 if up else cx + 1, body]
        elif what == 1:
            src = part_out.at[1 if up else 0]
            dst = part_in.at[0 if up else 1]
        else:
            src = p1.at[cx : cx + 2, body] if up else p1.at[4:6, body]
            dst = p1.at[0:2, body] if up else p1.at[cx + 4 : cx + 6, body]
        k = 3 * int(up) + what
        return pltpu.make_async_remote_copy(
            src_ref=src,
            dst_ref=dst,
            send_sem=rim_send.at[k],
            recv_sem=rim_recv.at[k],
            device_id={"gx": me + 1 if up else me - 1},
            device_id_type=MESH,
        )

    def send_rim(what):
        @pl.when(has_low)
        def _():
            rim(False, what).start()

        @pl.when(has_high)
        def _():
            rim(True, what).start()

    send_rim(0)
    for s in starts:
        o = pl.ds(s - PAD, ROWS)
        part_out[0, o] = scale * (flat_part(0, s) + prov[0, 2, at(s)])
        part_out[1, o] = scale * (flat_part(cx - 1, s) - prov[0, cx - 1, at(s)])
    send_rim(1)
    for p in range(1, cx - 1):
        for s in starts:
            p1[p + 3, at(s)] = scale * (
                flat_part(p, s) + prov[0, p + 2, at(s)] - prov[0, p, at(s)]
            )
    send_rim(2)
    for p in range(1, cx - 1):
        wrap(p1, p + 3)

    for what in range(3):

        @pl.when(has_low)
        def _():
            rim(True, what).wait_recv()

        @pl.when(has_high)
        def _():
            rim(False, what).wait_recv()

    for s in starts:
        o = pl.ds(s - PAD, ROWS)
        p1[3, at(s)] = part_out[0, o] - scale * prov[0, 0, at(s)]
        p1[cx + 2, at(s)] = part_out[1, o] + scale * prov[0, cx + 1, at(s)]
        p1[2, at(s)] = low_ok * (part_in[0, o] + scale * prov[0, 1, at(s)])
        p1[cx + 3, at(s)] = high_ok * (part_in[1, o] - scale * prov[0, cx, at(s)])
    for p in (1, 2, 3, cx + 2, cx + 3, cx + 4):
        wrap(p1, p)

    def sweep(old, new, back):
        planes = new.shape[0]
        outer = (planes - cx) // 2

        def plane(p, carry):
            ok = jnp.where(p < outer, low_ok, jnp.where(p >= outer + cx, high_ok, 1.0))
            for s in starts:
                centre = old[p + 1, at(s)]
                near = old[p, at(s)] + old[p + 2, at(s)]
                near = near + old[p + 1, at(s, 1)] + old[p + 1, at(s, -1)]
                near = near + deeper(centre) + shallower(centre)
                new[p, at(s)] = ok * (near * (1.0 / 6.0) + p1[p + back, at(s)])
            wrap(new, p)
            return carry

        lax.fori_loop(0, planes, plane, 0)

    sweep(p1, p2, 1)
    sweep(p2, p3, 2)

    def correct(p, carry):
        for s in starts:
            o = pl.ds(s - PAD, ROWS)
            centre = p3[p + 1, at(s)]
            out[0, p, o] = prov[0, p + 1, at(s)] - 0.5 * (p3[p + 2, at(s)] - p3[p, at(s)])
            out[1, p, o] = prov[1, p + 1, at(s)] - 0.5 * (
                p3[p + 1, at(s, 1)] - p3[p + 1, at(s, -1)]
            )
            out[2, p, o] = prov[2, p + 1, at(s)] - 0.5 * (deeper(centre) - shallower(centre))
        return carry

    lax.fori_loop(0, cx, correct, 0)

    def sent_blade(k, carry):
        blade(k, lax.rem(me + k, n), me).wait_send()
        return carry

    lax.fori_loop(1, n, sent_blade, 0)

    @pl.when(has_low)
    def _():
        feed(me).wait_send()
        halo(False).wait_send()
        for what in range(3):
            rim(False, what).wait_send()

    @pl.when(has_high)
    def _():
        halo(True).wait_send()
        for what in range(3):
            rim(True, what).wait_send()


def shards(n, velocity, inflow, blade_motion, blade_axis, blade_chord, host_cell, host_frac):
    cx, ny, nz = velocity.shape[1:]
    slots = host_cell.shape[0]
    high = PAD + ny + 8
    vmem = pltpu.VMEM
    f32 = jnp.float32
    dma = pltpu.SemaphoreType.DMA
    inside = pl.BlockSpec(memory_space=pltpu.VMEM)
    return pl.pallas_call(
        functools.partial(kernel, n),
        out_shape=jax.ShapeDtypeStruct(velocity.shape, f32),
        in_specs=[pl.BlockSpec(memory_space=pl.ANY)] + [inside] * 6,
        out_specs=inside,
        scratch_shapes=[
            vmem((3, cx + 4, high, nz), f32),
            vmem((cx + 2, high, nz), f32),
            vmem((3, cx + 2, high, nz), f32),
            vmem((cx + 6, high, nz), f32),
            vmem((cx + 4, high, nz), f32),
            vmem((cx + 2, high, nz), f32),
            vmem((2, ny, nz), f32),
            vmem((2, ny, nz), f32),
            vmem((16, slots), f32),
            vmem((n * SLOT // LANES, 8, LANES), f32),
            vmem((n * SLOT // 256, 8, 256), f32),
            vmem((n, 8, LANES), f32),
            vmem((n,) + inflow.shape, f32),
            dma,
            dma((2,)),
            dma((2,)),
            dma((n,)),
            dma((n,)),
            dma,
            dma((n,)),
            dma((6,)),
            dma((6,)),
        ],
        compiler_params=pltpu.CompilerParams(
            collective_id=0, has_side_effects=True, vmem_limit_bytes=48 * 1024 * 1024
        ),
    )(
        velocity,
        inflow,
        blade_motion,
        blade_axis,
        blade_chord.reshape(1, slots),
        host_cell.reshape(1, slots),
        host_frac,
    )


def solution(mesh):
    return jax.shard_map(
        functools.partial(shards, mesh.shape["gx"]),
        mesh=mesh,
        in_specs=(
            P("runs", "gx", None, None),
            P("runs", "gx", None),
            P("runs", "gx"),
            P("runs", "gx"),
            P(("runs", "gx")),
            P(("runs", "gx")),
            P("runs", "gx"),
        ),
        out_specs=P("runs", "gx", None, None),
        check_vma=False,
    )
```

time: 172 us -> 34.3 us (0.20)
  the two profiles are of different devices: /device:TPU:8 before, /device:TPU:9 now
where the time goes in v1:
time: 34.3 us; the launch traced here: 33.9 us
  Pallas kernels  28.5 us (83%)
  local copies, waits for them, and re-layouts  5.47 us (16%)
    pallas_call x1, Pallas kernels, shards(): pl.pallas_call(functools.partial(kernel, n), out_shape=jax.ShapeDtypeStru...  28.5 us
    unnamed x15, local copies, waits for them, and re-layouts  5.47 us

profile of v1, /device:TPU:9, one launch (start us, length us, event | category | flops | bytes accessed | tf_op | source)
XLA Modules:
  0.0 33.9 jit_solution(2259718539369361852)
XLA Ops:
  0.0 0.0 copy-start.6
  0.0 0.0 copy-start.5
  0.0 0.7 %copy-done.6 = s32[192]{0:T(256)S(1)} copy-done((s32[192]{0:T(256)S(1)}, s32[192]{0:T(256)}, u32[]{:S(2)}) %copy-start.6) | copy-done | bytes 792
  0.7 0.0 copy-done.5
  0.7 0.0 copy-start
  0.7 1.1 %copy-done = f32[3,4,128,128]{3,2,1,0:T(8,128)S(1)} copy-done((f32[3,4,128,128]{3,2,1,0:T(8,128)S(1)}, f32[3,4,128,128]{3,2,1,0:T(8,128)}, u32[]{:S(2)}) %copy-start) | copy-done | bytes 786456
  1.8 0.0 copy-start.1
  1.8 0.7 %copy-done.1 = f32[3,8,128]{2,1,0:T(8,128)S(1)} copy-done((f32[3,8,128]{2,1,0:T(8,128)S(1)}, f32[3,8,128]{2,1,0:T(8,128)}, u32[]{:S(2)}) %copy-start.1) | copy-done | bytes 12312
  2.5 0.0 copy-start.2
  2.5 0.7 %copy-done.2 = f32[3,192]{1,0:T(4,128)S(1)} copy-done((f32[3,192]{1,0:T(4,128)S(1)}, f32[3,192]{1,0:T(4,128)}, u32[]{:S(2)}) %copy-start.2) | copy-done | bytes 2328
  3.2 0.0 copy-start.3
  3.2 0.7 %copy-done.3 = f32[3,192]{1,0:T(4,128)S(1)} copy-done((f32[3,192]{1,0:T(4,128)S(1)}, f32[3,192]{1,0:T(4,128)}, u32[]{:S(2)}) %copy-start.3) | copy-done | bytes 2328
  3.9 0.0 copy-start.4
  3.9 0.7 %copy-done.4 = f32[3,192]{1,0:T(4,128)S(1)} copy-done((f32[3,192]{1,0:T(4,128)S(1)}, f32[3,192]{1,0:T(4,128)}, u32[]{:S(2)}) %copy-start.4) | copy-done | bytes 2328
  4.6 28.5 %shard_map.73 = f32[3,4,128,128]{3,2,1,0:T(8,128)S(1)} custom-call(f32[3,4,128,128]{3,2,1,0:T(8,128)S(1)} %copy-done, f32[3,8,128]{2,1,0:T(8,128)S(1)} %copy-done.1, f32[3,192]{1,0:T(4,128)S(1)} %copy-done.2, f32[3,192]{1,0:T(4,128)S(1)} %copy-done.3, f32[1,192]{1,0:T(1,128)S(1)} %bitcast.2, s32[1,192]{1,0:T(1,128)S(1)} %bitcast.3, f32[3,192]{1,0:T(4,128)S(1)} %copy-done.4), custom_call_target="tpu_custom_call" | custom-call | tf_op jit(solution)/shard_map/pallas_call | solution.py:480
  33.1 0.9 %copy.9 = f32[3,4,128,128]{3,2,1,0:T(8,128)} copy(f32[3,4,128,128]{3,2,1,0:T(8,128)S(1)} %shard_map.73) | data formatting | bytes 1572864
Async XLA Ops:
  0.0 0.7 %copy-start.6 = (s32[192]{0:T(256)S(1)}, s32[192]{0:T(256)}, u32[]{:S(2)}) copy-start(s32[192]{0:T(256)} %param.12) | copy-start | bytes 2308
  0.0 0.7 %copy-start.5 = (f32[192]{0:T(256)S(1)}, f32[192]{0:T(256)}, u32[]{:S(2)}) copy-start(f32[192]{0:T(256)} %param.11) | copy-start | bytes 2308
  0.7 1.1 %copy-start = (f32[3,4,128,128]{3,2,1,0:T(8,128)S(1)}, f32[3,4,128,128]{3,2,1,0:T(8,128)}, u32[]{:S(2)}) copy-start(f32[3,4,128,128]{3,2,1,0:T(8,128)} %vel.1) | copy-start | bytes 2359300
  1.8 0.7 %copy-start.1 = (f32[3,8,128]{2,1,0:T(8,128)S(1)}, f32[3,8,128]{2,1,0:T(8,128)}, u32[]{:S(2)}) copy-start(f32[3,8,128]{2,1,0:T(8,128)} %inflow.1) | copy-start | bytes 36868
  2.5 0.7 %copy-start.2 = (f32[3,192]{1,0:T(4,128)S(1)}, f32[3,192]{1,0:T(4,128)}, u32[]{:S(2)}) copy-start(f32[3,192]{1,0:T(4,128)} %motion.1) | copy-start | bytes 6916
  3.2 0.7 %copy-start.3 = (f32[3,192]{1,0:T(4,128)S(1)}, f32[3,192]{1,0:T(4,128)}, u32[]{:S(2)}) copy-start(f32[3,192]{1,0:T(4,128)} %axis.1) | copy-start | bytes 6916
  3.9 0.7 %copy-start.4 = (f32[3,192]{1,0:T(4,128)S(1)}, f32[3,192]{1,0:T(4,128)}, u32[]{:S(2)}) copy-start(f32[3,192]{1,0:T(4,128)} %frac.1) | copy-start | bytes 6916

commit v2 on v1

--- a/solution.py
+++ b/solution.py
@@ -43,6 +43,11 @@
     cell,
     frac,
     out,
+    motion_in,
+    axis_in,
+    chord_in,
+    cell_in,
+    frac_in,
     u,
     nu,
     prov,
@@ -57,14 +62,20 @@
     arrived,
     inlet,
     load_sem,
+    small_sem,
+    own_sem,
     halo_send,
     halo_recv,
     blade_send,
     blade_recv,
     in_send,
     in_recv,
+    nu_send,
+    nu_recv,
     rim_send,
     rim_recv,
+    result,
+    store_sem,
 ):
     me = lax.axis_index("gx")
     cx, ny, nz = vel.shape[1:]
@@ -83,16 +94,21 @@
         return carry
 
     lax.fori_loop(1, n, greet, 0)
-    load = pltpu.make_async_copy(vel, u.at[:, 2 : 2 + cx, body], load_sem)
+    pairs = (
+        (motion, motion_in),
+        (axis, axis_in),
+        (chord, chord_in),
+        (cell, cell_in),
+        (frac, frac_in),
+    )
+    small = [pltpu.make_async_copy(a, b, small_sem.at[k]) for k, (a, b) in enumerate(pairs)]
+    for copy in small:
+        copy.start()
+    load = pltpu.make_async_copy(vel, u.at[:, 1 : 1 + cx, body], load_sem)
     load.start()
 
     zeros = jnp.zeros((16, rows.shape[1]), jnp.float32)
     rows[...] = zeros
-    rows[0:3] = motion[...]
-    rows[3:6] = axis[...]
-    rows[6:7] = chord[...]
-    rows[8:9] = (cell[...] + 1).astype(jnp.float32)
-    rows[9:12] = frac[...]
     owners = 256 // SLOT
     wide = owners * cap
     source_lane = lax.broadcasted_iota(jnp.int32, (wide, 256), 0)
@@ -101,6 +117,13 @@
     picked = (source_lane == (slot_lane >> 4) * cap + within) & (within < cap)
     pick = jnp.where(picked, 1.0, 0.0)
     chunks = n // owners
+    for copy in small:
+        copy.wait()
+    rows[0:3] = motion_in[...]
+    rows[3:6] = axis_in[...]
+    rows[6:7] = chord_in[...]
+    rows[8:9] = (cell_in[...] + 1).astype(jnp.float32)
+    rows[9:12] = frac_in[...]
     for q in range(chunks):
         spaced = lax.dot_general(
             rows[:, q * wide : (q + 1) * wide],
@@ -115,9 +138,9 @@
 
     def halo(up):
         if up:
-            src, dst, to = vel.at[:, cx - 2 : cx], u.at[:, 0:2, body], me + 1
+            src, dst, to = vel.at[:, cx - 1], u.at[:, 0, body], me + 1
         else:
-            src, dst, to = vel.at[:, 0:2], u.at[:, cx + 2 : cx + 4, body], me - 1
+            src, dst, to = vel.at[:, 0], u.at[:, cx + 1, body], me - 1
         return pltpu.make_async_remote_copy(
             src_ref=src,
             dst_ref=dst,
@@ -169,7 +192,7 @@
 
     @pl.when(jnp.logical_not(has_high))
     def _():
-        u[:, cx + 2 : cx + 4] = jnp.zeros((3, 2) + u.shape[2:], jnp.float32)
+        u[:, cx + 1] = jnp.zeros((3,) + u.shape[2:], jnp.float32)
         prov[0, cx + 1] = jnp.zeros(prov.shape[2:], jnp.float32)
         p1[cx + 4 : cx + 6] = jnp.zeros((2,) + p1.shape[1:], jnp.float32)
         part_in[1] = jnp.zeros(part_in.shape[1:], jnp.float32)
@@ -187,7 +210,7 @@
     load.wait()
     for i in range(3):
         for x in range(cx):
-            wrap(u, i, x + 2)
+            wrap(u, i, x + 1)
 
     depth_bits, span_bits = nz.bit_length() - 1, ny.bit_length() - 1
     layer = lax.broadcasted_iota(jnp.int32, (LANES, 256), 0)
@@ -215,7 +238,7 @@
         for i in range(3):
             total = jnp.zeros((1, 256), jnp.float32)
             for x in range(cx):
-                lines = product(split(u[i, x + 2, body]), along_z, ((1,), (0,)))
+                lines = product(split(u[i, x + 1, body]), along_z, ((1,), (0,)))
                 total = total + along_x[x] * jnp.sum(lines * along_y, axis=0, keepdims=True)
             sampled.append(total)
 
@@ -257,33 +280,6 @@
                 else:
                     prov[i, x + 1, body] += laid
 
-    @pl.when(has_low)
-    def _():
-        halo(True).wait_recv()
-
-    @pl.when(has_high)
-    def _():
-        halo(False).wait_recv()
-
-    @pl.when(jnp.logical_not(has_low))
-    def _():
-        def take_inlet(k, carry):
-            feed(k).wait_recv()
-            return carry
-
-        lax.fori_loop(1, n, take_inlet, 0)
-        inlet[0] = inflow[...]
-        share = inflow.shape[1]
-        for k in range(n):
-            at = slice(PAD + k * share, PAD + (k + 1) * share)
-            for i in range(3):
-                u[i, 0, at] = inlet[k, i]
-                u[i, 1, at] = inlet[k, i]
-
-    for i in range(3):
-        wrap(u, i, 1)
-        wrap(u, i, cx + 2)
-
     first = lax.broadcasted_iota(jnp.int32, (ROWS, nz), 1) == 0
     last = lax.broadcasted_iota(jnp.int32, (ROWS, nz), 1) == nz - 1
 
@@ -298,15 +294,15 @@
     def at(start, shift=0):
         return pl.ds(start + shift, ROWS)
 
-    def viscosity(p, carry):
+    def viscosity(p, low, mid, up):
         for s in starts:
             d = []
             for i in range(3):
-                centre = u[i, p + 1, at(s)]
+                centre = u[i, mid, at(s)]
                 d.append(
                     (
-                        u[i, p + 2, at(s)] - u[i, p, at(s)],
-                        u[i, p + 1, at(s, 1)] - u[i, p + 1, at(s, -1)],
+                        u[i, up, at(s)] - u[i, low, at(s)],
+                        u[i, mid, at(s, 1)] - u[i, mid, at(s, -1)],
                         deeper(centre) - shallower(centre),
                     )
                 )
@@ -315,13 +311,74 @@
             shear = shear + shear + (xy * xy + xz * xz + yz * yz) + 4.0 * STRAIN_FLOOR
             nu[p, at(s)] = (0.25 * TIME_STEP * SMAGORINSKY) * jnp.sqrt(shear)
         wrap(nu, p)
+
+    def inner_viscosity(p, carry):
+        viscosity(p + 1, p, p + 1, p + 2)
         return carry
 
-    lax.fori_loop(0, cx + 2, viscosity, 0)
-
-    def momentum(p, carry):
+    lax.fori_loop(1, cx - 1, inner_viscosity, 0)
+
+    @pl.when(has_low)
+    def _():
+        halo(True).wait_recv()
+
+    @pl.when(has_high)
+    def _():
+        halo(False).wait_recv()
+
+    @pl.when(jnp.logical_not(has_low))
+    def _():
+        def take_inlet(k, carry):
+            feed(k).wait_recv()
+            return carry
+
+        lax.fori_loop(1, n, take_inlet, 0)
+        own = pltpu.make_async_copy(inflow, inlet.at[0], own_sem)
+        own.start()
+        own.wait()
+        share = inflow.shape[1]
+        for k in range(n):
+            at = slice(PAD + k * share, PAD + (k + 1) * share)
+            for i in range(3):
+                u[i, 0, at] = inlet[k, i]
+
+    for i in range(3):
+        wrap(u, i, 0)
+        wrap(u, i, cx + 1)
+
+    def layer_of(up):
+        return pltpu.make_async_remote_copy(
+            src_ref=nu.at[cx if up else 1, body],
+            dst_ref=nu.at[0 if up else cx + 1, body],
+            send_sem=nu_send.at[int(up)],
+            recv_sem=nu_recv.at[int(up)],
+            device_id={"gx": me + 1 if up else me - 1},
+            device_id_type=MESH,
+        )
+
+    viscosity(1, 0, 1, 2)
+
+    @pl.when(has_low)
+    def _():
+        layer_of(False).start()
+
+    viscosity(cx, cx - 1, cx, cx + 1)
+
+    @pl.when(has_high)
+    def _():
+        layer_of(True).start()
+
+    @pl.when(jnp.logical_not(has_low))
+    def _():
+        viscosity(0, 0, 0, 1)
+
+    @pl.when(jnp.logical_not(has_high))
+    def _():
+        viscosity(cx + 1, cx, cx + 1, cx + 1)
+
+    def momentum(p):
         for s in starts:
-            centre = [u[i, p + 2, at(s)] for i in range(3)]
+            centre = [u[i, p + 1, at(s)] for i in range(3)]
             own = nu[p + 1, at(s)]
             edge = centre[2] * centre[2]
             edge = edge + edge + centre[0] * centre[0] + centre[1] * centre[1]
@@ -338,14 +395,17 @@
             rest = 1.0 - (coef[0] + coef[1] + coef[2] + coef[3] + coef[4] + coef[5])
             for i in range(3):
                 value = prov[i, p + 1, at(s)] + rest * centre[i]
-                value = value + coef[0] * u[i, p + 3, at(s)] + coef[1] * u[i, p + 1, at(s)]
-                value = value + coef[2] * u[i, p + 2, at(s, 1)] + coef[3] * u[i, p + 2, at(s, -1)]
+                value = value + coef[0] * u[i, p + 2, at(s)] + coef[1] * u[i, p, at(s)]
+                value = value + coef[2] * u[i, p + 1, at(s, 1)] + coef[3] * u[i, p + 1, at(s, -1)]
                 value = value + coef[4] * deeper(centre[i]) + coef[5] * shallower(centre[i])
                 prov[i, p + 1, at(s)] = value
         wrap(prov, 1, p + 1)
+
+    def inner_momentum(p, carry):
+        momentum(p)
         return carry
 
-    lax.fori_loop(0, cx, momentum, 0)
+    lax.fori_loop(1, cx - 1, inner_momentum, 0)
 
     scale = -1.0 / 12.0
 
@@ -361,9 +421,10 @@
             src = part_out.at[1 if up else 0]
             dst = part_in.at[0 if up else 1]
         else:
-            src = p1.at[cx : cx + 2, body] if up else p1.at[4:6, body]
-            dst = p1.at[0:2, body] if up else p1.at[cx + 4 : cx + 6, body]
-        k = 3 * int(up) + what
+            plane = cx - 5 + what if up else what - 1
+            src = p1.at[plane + 3, body]
+            dst = p1.at[plane + 3 - cx if up else plane + 3 + cx, body]
+        k = 4 * int(up) + what
         return pltpu.make_async_remote_copy(
             src_ref=src,
             dst_ref=dst,
@@ -373,31 +434,49 @@
             device_id_type=MESH,
         )
 
-    def send_rim(what):
-        @pl.when(has_low)
+    def send_rim(up, what):
+        @pl.when(has_high if up else has_low)
         def _():
-            rim(False, what).start()
-
-        @pl.when(has_high)
-        def _():
-            rim(True, what).start()
-
-    send_rim(0)
-    for s in starts:
-        o = pl.ds(s - PAD, ROWS)
-        part_out[0, o] = scale * (flat_part(0, s) + prov[0, 2, at(s)])
-        part_out[1, o] = scale * (flat_part(cx - 1, s) - prov[0, cx - 1, at(s)])
-    send_rim(1)
-    for p in range(1, cx - 1):
+            rim(up, what).start()
+
+    def first_potential(p):
         for s in starts:
             p1[p + 3, at(s)] = scale * (
                 flat_part(p, s) + prov[0, p + 2, at(s)] - prov[0, p, at(s)]
             )
-    send_rim(2)
+
+    @pl.when(has_low)
+    def _():
+        layer_of(True).wait_recv()
+
+    momentum(0)
+    send_rim(False, 0)
+    for s in starts:
+        part_out[0, pl.ds(s - PAD, ROWS)] = scale * (flat_part(0, s) + prov[0, 2, at(s)])
+    send_rim(False, 1)
+    for p in range(1, cx - 2):
+        first_potential(p)
+    send_rim(False, 2)
+    send_rim(True, 2)
+
+    @pl.when(has_high)
+    def _():
+        layer_of(False).wait_recv()
+
+    momentum(cx - 1)
+    send_rim(True, 0)
+    for s in starts:
+        part_out[1, pl.ds(s - PAD, ROWS)] = scale * (
+            flat_part(cx - 1, s) - prov[0, cx - 1, at(s)]
+        )
+    send_rim(True, 1)
+    first_potential(cx - 2)
+    send_rim(False, 3)
+    send_rim(True, 3)
     for p in range(1, cx - 1):
         wrap(p1, p + 3)
 
-    for what in range(3):
+    for what in range(4):
 
         @pl.when(has_low)
         def _():
@@ -436,15 +515,19 @@
     sweep(p1, p2, 1)
     sweep(p2, p3, 2)
 
+    def store(p):
+        return pltpu.make_async_copy(result.at[:, p], out.at[:, p], store_sem.at[p])
+
     def correct(p, carry):
         for s in starts:
             o = pl.ds(s - PAD, ROWS)
             centre = p3[p + 1, at(s)]
-            out[0, p, o] = prov[0, p + 1, at(s)] - 0.5 * (p3[p + 2, at(s)] - p3[p, at(s)])
-            out[1, p, o] = prov[1, p + 1, at(s)] - 0.5 * (
+            result[0, p, o] = prov[0, p + 1, at(s)] - 0.5 * (p3[p + 2, at(s)] - p3[p, at(s)])
+            result[1, p, o] = prov[1, p + 1, at(s)] - 0.5 * (
                 p3[p + 1, at(s, 1)] - p3[p + 1, at(s, -1)]
             )
-            out[2, p, o] = prov[2, p + 1, at(s)] - 0.5 * (deeper(centre) - shallower(centre))
+            result[2, p, o] = prov[2, p + 1, at(s)] - 0.5 * (deeper(centre) - shallower(centre))
+        store(p).start()
         return carry
 
     lax.fori_loop(0, cx, correct, 0)
@@ -454,18 +537,22 @@
         return carry
 
     lax.fori_loop(1, n, sent_blade, 0)
+    for p in range(cx):
+        store(p).wait()
 
     @pl.when(has_low)
     def _():
         feed(me).wait_send()
         halo(False).wait_send()
-        for what in range(3):
+        layer_of(False).wait_send()
+        for what in range(4):
             rim(False, what).wait_send()
 
     @pl.when(has_high)
     def _():
         halo(True).wait_send()
-        for what in range(3):
+        layer_of(True).wait_send()
+        for what in range(4):
             rim(True, what).wait_send()
 
 
@@ -476,14 +563,18 @@
     vmem = pltpu.VMEM
     f32 = jnp.float32
     dma = pltpu.SemaphoreType.DMA
-    inside = pl.BlockSpec(memory_space=pltpu.VMEM)
     return pl.pallas_call(
         functools.partial(kernel, n),
         out_shape=jax.ShapeDtypeStruct(velocity.shape, f32),
-        in_specs=[pl.BlockSpec(memory_space=pl.ANY)] + [inside] * 6,
-        out_specs=inside,
+        in_specs=[pl.BlockSpec(memory_space=pltpu.HBM)] * 7,
+        out_specs=pl.BlockSpec(memory_space=pltpu.HBM),
         scratch_shapes=[
-            vmem((3, cx + 4, high, nz), f32),
+            vmem((3, slots), f32),
+            vmem((3, slots), f32),
+            vmem((1, slots), f32),
+            vmem((1, slots), jnp.int32),
+            vmem((3, slots), f32),
+            vmem((3, cx + 2, high, nz), f32),
             vmem((cx + 2, high, nz), f32),
             vmem((3, cx + 2, high, nz), f32),
             vmem((cx + 6, high, nz), f32),
@@ -497,17 +588,23 @@
             vmem((n, 8, LANES), f32),
             vmem((n,) + inflow.shape, f32),
             dma,
+            dma((5,)),
+            dma,
             dma((2,)),
             dma((2,)),
             dma((n,)),
             dma((n,)),
             dma,
             dma((n,)),
-            dma((6,)),
-            dma((6,)),
+            dma((2,)),
+            dma((2,)),
+            dma((8,)),
+            dma((8,)),
+            vmem(velocity.shape, f32),
+            dma((cx,)),
         ],
         compiler_params=pltpu.CompilerParams(
-            collective_id=0, has_side_effects=True, vmem_limit_bytes=48 * 1024 * 1024
+            collective_id=0, has_side_effects=True, vmem_limit_bytes=64 * 1024 * 1024 - 65536
         ),
     )(
         velocity,

time: 34.3 us -> 28.8 us (0.84)
  local copies, waits for them, and re-layouts: 5.47 us -> 2.06 us
  Pallas kernels: 28.5 us -> 26.5 us
    unnamed x15 -> x1, local copies, waits for them, and re-layouts: 5.47 us -> 2.06 us
    pallas_call x1, Pallas kernels: 28.5 us -> 26.5 us  [shards(): pl.pallas_call(functools.partial(kernel, n), out_shape=jax.ShapeDtypeStru...]
where the time goes in v2:
time: 28.8 us; the launch traced here: 28.5 us
  Pallas kernels  26.5 us (92%)
  local copies, waits for them, and re-layouts  2.06 us (7%)
    pallas_call x1, Pallas kernels, shards(): pl.pallas_call(functools.partial(kernel, n), out_shape=jax.ShapeDtypeStru...  26.5 us
    unnamed x1, local copies, waits for them, and re-layouts  2.06 us

profile of v2, /device:TPU:9, one launch (start us, length us, event | category | flops | bytes accessed | tf_op | source)
XLA Modules:
  0.0 28.5 jit_solution(4019325201000567291)
XLA Ops:
  0.0 26.5 %shard_map.73 = f32[3,4,128,128]{3,2,1,0:T(8,128)} custom-call(f32[3,4,128,128]{3,2,1,0:T(8,128)} %vel.1, f32[3,8,128]{2,1,0:T(8,128)} %inflow.1, f32[3,192]{1,0:T(4,128)} %motion.1, f32[3,192]{1,0:T(4,128)} %axis.1, f32[1,192]{1,0:T(1,128)} %bitcast.2, s32[1,192]{1,0:T(1,128)} %bitcast.3, f32[3,192]{1,0:T(4,128)} %frac.1), custom_call_target="tpu_custom_call" | custom-call | tf_op jit(solution)/shard_map/pallas_call | solution.py:566
  26.5 2.1 %copy.9 = f32[3,4,128,128]{3,2,1,0:T(8,128)} copy(f32[3,4,128,128]{3,2,1,0:T(8,128)} %shard_map.73) | data formatting | bytes 1572864

commit v3 on v2

--- a/solution.py
+++ b/solution.py
@@ -42,7 +42,8 @@
     chord,
     cell,
     frac,
-    out,
+    given,
+    change,
     motion_in,
     axis_in,
     chord_in,
@@ -75,6 +76,7 @@
     rim_send,
     rim_recv,
     result,
+    keep_sem,
     store_sem,
 ):
     me = lax.axis_index("gx")
@@ -106,6 +108,54 @@
         copy.start()
     load = pltpu.make_async_copy(vel, u.at[:, 1 : 1 + cx, body], load_sem)
     load.start()
+
+    def halo(up):
+        if up:
+            src, dst, to = vel.at[:, cx - 1], u.at[:, 0, body], me + 1
+        else:
+            src, dst, to = vel.at[:, 0], u.at[:, cx + 1, body], me - 1
+        return pltpu.make_async_remote_copy(
+            src_ref=src,
+            dst_ref=dst,
+            send_sem=halo_send.at[int(up)],
+            recv_sem=halo_recv.at[int(up)],
+            device_id={"gx": to},
+            device_id_type=MESH,
+        )
+
+    def feed(slot):
+        return pltpu.make_async_remote_copy(
+            src_ref=inflow,
+            dst_ref=inlet.at[slot],
+            send_sem=in_send,
+            recv_sem=in_recv.at[slot],
+            device_id={"gx": 0},
+            device_id_type=MESH,
+        )
+
+    @pl.when(jnp.logical_not(has_high))
+    def _():
+        u[:, cx + 1] = jnp.zeros((3,) + u.shape[2:], jnp.float32)
+        prov[0, cx + 1] = jnp.zeros(prov.shape[2:], jnp.float32)
+        p1[cx + 4 : cx + 6] = jnp.zeros((2,) + p1.shape[1:], jnp.float32)
+        part_in[1] = jnp.zeros(part_in.shape[1:], jnp.float32)
+
+    @pl.when(jnp.logical_not(has_low))
+    def _():
+        prov[0, 0] = jnp.zeros(prov.shape[2:], jnp.float32)
+        p1[0:2] = jnp.zeros((2,) + p1.shape[1:], jnp.float32)
+        part_in[0] = jnp.zeros(part_in.shape[1:], jnp.float32)
+
+    pl.semaphore_wait(barrier, n - 1)
+
+    @pl.when(has_low)
+    def _():
+        feed(me).start()
+        halo(False).start()
+
+    @pl.when(has_high)
+    def _():
+        halo(True).start()
 
     zeros = jnp.zeros((16, rows.shape[1]), jnp.float32)
     rows[...] = zeros
@@ -136,20 +186,6 @@
         for h in range(256 // LANES):
             blocks[q * (256 // LANES) + h] = spaced[0:8, h * LANES : (h + 1) * LANES]
 
-    def halo(up):
-        if up:
-            src, dst, to = vel.at[:, cx - 1], u.at[:, 0, body], me + 1
-        else:
-            src, dst, to = vel.at[:, 0], u.at[:, cx + 1, body], me - 1
-        return pltpu.make_async_remote_copy(
-            src_ref=src,
-            dst_ref=dst,
-            send_sem=halo_send.at[int(up)],
-            recv_sem=halo_recv.at[int(up)],
-            device_id={"gx": to},
-            device_id_type=MESH,
-        )
-
     per = LANES // SLOT
 
     def blade(k, to, slot):
@@ -162,46 +198,12 @@
             device_id_type=MESH,
         )
 
-    def feed(slot):
-        return pltpu.make_async_remote_copy(
-            src_ref=inflow,
-            dst_ref=inlet.at[slot],
-            send_sem=in_send,
-            recv_sem=in_recv.at[slot],
-            device_id={"gx": 0},
-            device_id_type=MESH,
-        )
-
-    pl.semaphore_wait(barrier, n - 1)
-
-    @pl.when(has_low)
-    def _():
-        feed(me).start()
-        halo(False).start()
-
-    @pl.when(has_high)
-    def _():
-        halo(True).start()
-
     def send_blade(k, carry):
         blade(k, lax.rem(me + k, n), me).start()
         return carry
 
     lax.fori_loop(1, n, send_blade, 0)
     arrived[me] = blocks[me // per]
-
-    @pl.when(jnp.logical_not(has_high))
-    def _():
-        u[:, cx + 1] = jnp.zeros((3,) + u.shape[2:], jnp.float32)
-        prov[0, cx + 1] = jnp.zeros(prov.shape[2:], jnp.float32)
-        p1[cx + 4 : cx + 6] = jnp.zeros((2,) + p1.shape[1:], jnp.float32)
-        part_in[1] = jnp.zeros(part_in.shape[1:], jnp.float32)
-
-    @pl.when(jnp.logical_not(has_low))
-    def _():
-        prov[0, 0] = jnp.zeros(prov.shape[2:], jnp.float32)
-        p1[0:2] = jnp.zeros((2,) + p1.shape[1:], jnp.float32)
-        part_in[0] = jnp.zeros(part_in.shape[1:], jnp.float32)
 
     def wrap(ref, *lead):
         ref[(*lead, slice(PAD - 1, PAD))] = ref[(*lead, slice(PAD + ny - 1, PAD + ny))]
@@ -241,6 +243,102 @@
                 lines = product(split(u[i, x + 1, body]), along_z, ((1,), (0,)))
                 total = total + along_x[x] * jnp.sum(lines * along_y, axis=0, keepdims=True)
             sampled.append(total)
+
+    first = lax.broadcasted_iota(jnp.int32, (ROWS, nz), 1) == 0
+    last = lax.broadcasted_iota(jnp.int32, (ROWS, nz), 1) == nz - 1
+
+    def deeper(value, edge=0.0):
+        return jnp.where(last, edge, pltpu.roll(value, nz - 1, 1))
+
+    def shallower(value, edge=0.0):
+        return jnp.where(first, edge, pltpu.roll(value, 1, 1))
+
+    starts = range(PAD, PAD + ny, ROWS)
+
+    def at(start, shift=0):
+        return pl.ds(start + shift, ROWS)
+
+    def viscosity(p, low, mid, up):
+        for s in starts:
+            d = []
+            for i in range(3):
+                centre = u[i, mid, at(s)]
+                d.append(
+                    (
+                        u[i, up, at(s)] - u[i, low, at(s)],
+                        u[i, mid, at(s, 1)] - u[i, mid, at(s, -1)],
+                        deeper(centre) - shallower(centre),
+                    )
+                )
+            xy, xz, yz = d[0][1] + d[1][0], d[0][2] + d[2][0], d[1][2] + d[2][1]
+            shear = d[0][0] * d[0][0] + d[1][1] * d[1][1] + d[2][2] * d[2][2]
+            shear = shear + shear + (xy * xy + xz * xz + yz * yz) + 4.0 * STRAIN_FLOOR
+            nu[p, at(s)] = (0.25 * TIME_STEP * SMAGORINSKY) * jnp.sqrt(shear)
+        wrap(nu, p)
+
+    def inner_viscosity(p, carry):
+        viscosity(p + 1, p, p + 1, p + 2)
+        return carry
+
+    lax.fori_loop(1, cx - 1, inner_viscosity, 0)
+
+    @pl.when(has_low)
+    def _():
+        halo(True).wait_recv()
+
+    @pl.when(has_high)
+    def _():
+        halo(False).wait_recv()
+
+    @pl.when(jnp.logical_not(has_low))
+    def _():
+        def take_inlet(k, carry):
+            feed(k).wait_recv()
+            return carry
+
+        lax.fori_loop(1, n, take_inlet, 0)
+        own = pltpu.make_async_copy(inflow, inlet.at[0], own_sem)
+        own.start()
+        own.wait()
+        share = inflow.shape[1]
+        for k in range(n):
+            at = slice(PAD + k * share, PAD + (k + 1) * share)
+            for i in range(3):
+                u[i, 0, at] = inlet[k, i]
+
+    for i in range(3):
+        wrap(u, i, 0)
+        wrap(u, i, cx + 1)
+
+    def layer_of(up):
+        return pltpu.make_async_remote_copy(
+            src_ref=nu.at[cx if up else 1, body],
+            dst_ref=nu.at[0 if up else cx + 1, body],
+            send_sem=nu_send.at[int(up)],
+            recv_sem=nu_recv.at[int(up)],
+            device_id={"gx": me + 1 if up else me - 1},
+            device_id_type=MESH,
+        )
+
+    viscosity(1, 0, 1, 2)
+
+    @pl.when(has_low)
+    def _():
+        layer_of(False).start()
+
+    viscosity(cx, cx - 1, cx, cx + 1)
+
+    @pl.when(has_high)
+    def _():
+        layer_of(True).start()
+
+    @pl.when(jnp.logical_not(has_low))
+    def _():
+        viscosity(0, 0, 0, 1)
+
+    @pl.when(jnp.logical_not(has_high))
+    def _():
+        viscosity(cx + 1, cx, cx + 1, cx + 1)
 
     def take_blade(k, carry):
         blade(k, me, lax.rem(me + n - k, n)).wait_recv()
@@ -280,102 +378,6 @@
                 else:
                     prov[i, x + 1, body] += laid
 
-    first = lax.broadcasted_iota(jnp.int32, (ROWS, nz), 1) == 0
-    last = lax.broadcasted_iota(jnp.int32, (ROWS, nz), 1) == nz - 1
-
-    def deeper(value, edge=0.0):
-        return jnp.where(last, edge, pltpu.roll(value, nz - 1, 1))
-
-    def shallower(value, edge=0.0):
-        return jnp.where(first, edge, pltpu.roll(value, 1, 1))
-
-    starts = range(PAD, PAD + ny, ROWS)
-
-    def at(start, shift=0):
-        return pl.ds(start + shift, ROWS)
-
-    def viscosity(p, low, mid, up):
-        for s in starts:
-            d = []
-            for i in range(3):
-                centre = u[i, mid, at(s)]
-                d.append(
-                    (
-                        u[i, up, at(s)] - u[i, low, at(s)],
-                        u[i, mid, at(s, 1)] - u[i, mid, at(s, -1)],
-                        deeper(centre) - shallower(centre),
-                    )
-                )
-            xy, xz, yz = d[0][1] + d[1][0], d[0][2] + d[2][0], d[1][2] + d[2][1]
-            shear = d[0][0] * d[0][0] + d[1][1] * d[1][1] + d[2][2] * d[2][2]
-            shear = shear + shear + (xy * xy + xz * xz + yz * yz) + 4.0 * STRAIN_FLOOR
-            nu[p, at(s)] = (0.25 * TIME_STEP * SMAGORINSKY) * jnp.sqrt(shear)
-        wrap(nu, p)
-
-    def inner_viscosity(p, carry):
-        viscosity(p + 1, p, p + 1, p + 2)
-        return carry
-
-    lax.fori_loop(1, cx - 1, inner_viscosity, 0)
-
-    @pl.when(has_low)
-    def _():
-        halo(True).wait_recv()
-
-    @pl.when(has_high)
-    def _():
-        halo(False).wait_recv()
-
-    @pl.when(jnp.logical_not(has_low))
-    def _():
-        def take_inlet(k, carry):
-            feed(k).wait_recv()
-            return carry
-
-        lax.fori_loop(1, n, take_inlet, 0)
-        own = pltpu.make_async_copy(inflow, inlet.at[0], own_sem)
-        own.start()
-        own.wait()
-        share = inflow.shape[1]
-        for k in range(n):
-            at = slice(PAD + k * share, PAD + (k + 1) * share)
-            for i in range(3):
-                u[i, 0, at] = inlet[k, i]
-
-    for i in range(3):
-        wrap(u, i, 0)
-        wrap(u, i, cx + 1)
-
-    def layer_of(up):
-        return pltpu.make_async_remote_copy(
-            src_ref=nu.at[cx if up else 1, body],
-            dst_ref=nu.at[0 if up else cx + 1, body],
-            send_sem=nu_send.at[int(up)],
-            recv_sem=nu_recv.at[int(up)],
-            device_id={"gx": me + 1 if up else me - 1},
-            device_id_type=MESH,
-        )
-
-    viscosity(1, 0, 1, 2)
-
-    @pl.when(has_low)
-    def _():
-        layer_of(False).start()
-
-    viscosity(cx, cx - 1, cx, cx + 1)
-
-    @pl.when(has_high)
-    def _():
-        layer_of(True).start()
-
-    @pl.when(jnp.logical_not(has_low))
-    def _():
-        viscosity(0, 0, 0, 1)
-
-    @pl.when(jnp.logical_not(has_high))
-    def _():
-        viscosity(cx + 1, cx, cx + 1, cx + 1)
-
     def momentum(p):
         for s in starts:
             centre = [u[i, p + 1, at(s)] for i in range(3)]
@@ -473,6 +475,8 @@
     first_potential(cx - 2)
     send_rim(False, 3)
     send_rim(True, 3)
+    keep = pltpu.make_async_copy(prov.at[:, 1 : 1 + cx, body], given, keep_sem)
+    keep.start()
     for p in range(1, cx - 1):
         wrap(p1, p + 3)
 
@@ -516,17 +520,15 @@
     sweep(p2, p3, 2)
 
     def store(p):
-        return pltpu.make_async_copy(result.at[:, p], out.at[:, p], store_sem.at[p])
+        return pltpu.make_async_copy(result.at[:, p], change.at[:, p], store_sem.at[p])
 
     def correct(p, carry):
         for s in starts:
             o = pl.ds(s - PAD, ROWS)
             centre = p3[p + 1, at(s)]
-            result[0, p, o] = prov[0, p + 1, at(s)] - 0.5 * (p3[p + 2, at(s)] - p3[p, at(s)])
-            result[1, p, o] = prov[1, p + 1, at(s)] - 0.5 * (
-                p3[p + 1, at(s, 1)] - p3[p + 1, at(s, -1)]
-            )
-            result[2, p, o] = prov[2, p + 1, at(s)] - 0.5 * (deeper(centre) - shallower(centre))
+            result[0, p, o] = 0.5 * (p3[p + 2, at(s)] - p3[p, at(s)])
+            result[1, p, o] = 0.5 * (p3[p + 1, at(s, 1)] - p3[p + 1, at(s, -1)])
+            result[2, p, o] = 0.5 * (deeper(centre) - shallower(centre))
         store(p).start()
         return carry
 
@@ -537,6 +539,7 @@
         return carry
 
     lax.fori_loop(1, n, sent_blade, 0)
+    keep.wait()
     for p in range(cx):
         store(p).wait()
 
@@ -563,11 +566,11 @@
     vmem = pltpu.VMEM
     f32 = jnp.float32
     dma = pltpu.SemaphoreType.DMA
-    return pl.pallas_call(
+    provisional, gradient = pl.pallas_call(
         functools.partial(kernel, n),
-        out_shape=jax.ShapeDtypeStruct(velocity.shape, f32),
+        out_shape=[jax.ShapeDtypeStruct(velocity.shape, f32)] * 2,
         in_specs=[pl.BlockSpec(memory_space=pltpu.HBM)] * 7,
-        out_specs=pl.BlockSpec(memory_space=pltpu.HBM),
+        out_specs=[pl.BlockSpec(memory_space=pltpu.HBM)] * 2,
         scratch_shapes=[
             vmem((3, slots), f32),
             vmem((3, slots), f32),
@@ -601,6 +604,7 @@
             dma((8,)),
             dma((8,)),
             vmem(velocity.shape, f32),
+            dma,
             dma((cx,)),
         ],
         compiler_params=pltpu.CompilerParams(
@@ -615,6 +619,7 @@
         host_cell.reshape(1, slots),
         host_frac,
     )
+    return provisional - gradient
 
 
 def solution(mesh):

time: 28.8 us -> 27.4 us (0.951)
  the two profiles are of different devices: /device:TPU:9 before, /device:TPU:2 now
where the time goes in v3:
time: 27.4 us; the launch traced here: 27.2 us
  Pallas kernels  24.8 us (91%)
  other arithmetic  2.33 us (9%)
    pallas_call x1, Pallas kernels, shards(): pl.pallas_call(functools.partial(kernel, n), out_shape=[jax.ShapeDtypeStr...  24.8 us
    sub x1, other arithmetic, shards(): return provisional - gradient  2.33 us

profile of v3, /device:TPU:2, one launch (start us, length us, event | category | flops | bytes accessed | tf_op | source)
XLA Modules:
  0.0 27.2 jit_solution(9749516928059622608)
XLA Ops:
  0.0 24.8 %shard_map.73 = (f32[3,4,128,128]{3,2,1,0:T(8,128)}, f32[3,4,128,128]{3,2,1,0:T(8,128)}) custom-call(f32[3,4,128,128]{3,2,1,0:T(8,128)} %vel.1, f32[3,8,128]{2,1,0:T(8,128)} %inflow.1, f32[3,192]{1,0:T(4,128)} %motion.1, f32[3,192]{1,0:T(4,128)} %axis.1, f32[1,192]{1,0:T(1,128)} %bitcast.2, s32[1,192]{1,0:T(1,128)} %bitcast.3, f32[3,192]{1,0:T(4,128)} %frac.1), custom_call_target="tpu_custom_call" | custom-call | tf_op jit(solution)/shard_map/pallas_call | solution.py:569
  24.8 2.3 %sub.3 = f32[3,4,128,128]{3,2,1,0:T(8,128)} subtract(f32[3,4,128,128]{3,2,1,0:T(8,128)} %get-tuple-element.7, f32[3,4,128,128]{3,2,1,0:T(8,128)} %get-tuple-element.8) | non-fusion elementwise | flops 196608 | bytes 2359296 | tf_op jit(solution)/shard_map/sub | solution.py:622

commit v4 on v3

--- a/solution.py
+++ b/solution.py
@@ -43,7 +43,7 @@
     cell,
     frac,
     given,
-    change,
+    potential,
     motion_in,
     axis_in,
     chord_in,
@@ -75,7 +75,6 @@
     nu_recv,
     rim_send,
     rim_recv,
-    result,
     keep_sem,
     store_sem,
 ):
@@ -499,7 +498,10 @@
     for p in (1, 2, 3, cx + 2, cx + 3, cx + 4):
         wrap(p1, p)
 
-    def sweep(old, new, back):
+    def store(p):
+        return pltpu.make_async_copy(p3.at[p], potential.at[p], store_sem.at[p])
+
+    def sweep(old, new, back, done=None):
         planes = new.shape[0]
         outer = (planes - cx) // 2
 
@@ -512,27 +514,14 @@
                 near = near + deeper(centre) + shallower(centre)
                 new[p, at(s)] = ok * (near * (1.0 / 6.0) + p1[p + back, at(s)])
             wrap(new, p)
+            if done is not None:
+                done(p)
             return carry
 
         lax.fori_loop(0, planes, plane, 0)
 
     sweep(p1, p2, 1)
-    sweep(p2, p3, 2)
-
-    def store(p):
-        return pltpu.make_async_copy(result.at[:, p], change.at[:, p], store_sem.at[p])
-
-    def correct(p, carry):
-        for s in starts:
-            o = pl.ds(s - PAD, ROWS)
-            centre = p3[p + 1, at(s)]
-            result[0, p, o] = 0.5 * (p3[p + 2, at(s)] - p3[p, at(s)])
-            result[1, p, o] = 0.5 * (p3[p + 1, at(s, 1)] - p3[p + 1, at(s, -1)])
-            result[2, p, o] = 0.5 * (deeper(centre) - shallower(centre))
-        store(p).start()
-        return carry
-
-    lax.fori_loop(0, cx, correct, 0)
+    sweep(p2, p3, 2, lambda p: store(p).start())
 
     def sent_blade(k, carry):
         blade(k, lax.rem(me + k, n), me).wait_send()
@@ -540,7 +529,7 @@
 
     lax.fori_loop(1, n, sent_blade, 0)
     keep.wait()
-    for p in range(cx):
+    for p in range(cx + 2):
         store(p).wait()
 
     @pl.when(has_low)
@@ -557,6 +546,21 @@
         layer_of(True).wait_send()
         for what in range(4):
             rim(True, what).wait_send()
+
+
+def correct(given, below, here, above, out):
+    ny, nz = given.shape[2:]
+    spot = lax.broadcasted_iota(jnp.int32, (ROWS, nz), 1)
+    for s in range(0, ny, ROWS):
+        o = pl.ds(s, ROWS)
+        row = pl.ds(PAD + s, ROWS)
+        centre = here[0, row]
+        deeper = jnp.where(spot == nz - 1, 0.0, pltpu.roll(centre, nz - 1, 1))
+        shallower = jnp.where(spot == 0, 0.0, pltpu.roll(centre, 1, 1))
+        along_y = here[0, pl.ds(PAD + s + 1, ROWS)] - here[0, pl.ds(PAD + s - 1, ROWS)]
+        out[0, 0, o] = given[0, 0, o] - 0.5 * (above[0, row] - below[0, row])
+        out[1, 0, o] = given[1, 0, o] - 0.5 * along_y
+        out[2, 0, o] = given[2, 0, o] - 0.5 * (deeper - shallower)
 
 
 def shards(n, velocity, inflow, blade_motion, blade_axis, blade_chord, host_cell, host_frac):
@@ -566,9 +570,12 @@
     vmem = pltpu.VMEM
     f32 = jnp.float32
     dma = pltpu.SemaphoreType.DMA
-    provisional, gradient = pl.pallas_call(
+    provisional, potential = pl.pallas_call(
         functools.partial(kernel, n),
-        out_shape=[jax.ShapeDtypeStruct(velocity.shape, f32)] * 2,
+        out_shape=[
+            jax.ShapeDtypeStruct(velocity.shape, f32),
+            jax.ShapeDtypeStruct((cx + 2, high, nz), f32),
+        ],
         in_specs=[pl.BlockSpec(memory_space=pltpu.HBM)] * 7,
         out_specs=[pl.BlockSpec(memory_space=pltpu.HBM)] * 2,
         scratch_shapes=[
@@ -603,9 +610,8 @@
             dma((2,)),
             dma((8,)),
             dma((8,)),
-            vmem(velocity.shape, f32),
             dma,
-            dma((cx,)),
+            dma((cx + 2,)),
         ],
         compiler_params=pltpu.CompilerParams(
             collective_id=0, has_side_effects=True, vmem_limit_bytes=64 * 1024 * 1024 - 65536
@@ -619,7 +625,16 @@
         host_cell.reshape(1, slots),
         host_frac,
     )
-    return provisional - gradient
+    block = pl.BlockSpec((3, 1, ny, nz), lambda p: (0, p, 0, 0))
+    near = [pl.BlockSpec((1, high, nz), lambda p, k=k: (p + k, 0, 0)) for k in range(3)]
+    return pl.pallas_call(
+        correct,
+        out_shape=jax.ShapeDtypeStruct(velocity.shape, f32),
+        grid=(cx,),
+        in_specs=[block] + near,
+        out_specs=block,
+        compiler_params=pltpu.CompilerParams(vmem_limit_bytes=64 * 1024 * 1024 - 65536),
+    )(provisional, potential, potential, potential)
 
 
 def solution(mesh):

time: 27.4 us -> 28.3 us (1.033)
  Pallas kernels: 24.8 us -> 28.1 us
  other arithmetic: 2.33 us -> 0 us
    pallas_call x0 -> x1, Pallas kernels: none -> 3.72 us  [shards(): pl.pallas_call(correct, out_shape=jax.ShapeDtypeStruct(velocity.shape, f3...]
    sub x1 -> x0, other arithmetic: 2.33 us -> none  [shards(): return provisional - gradient]
    pallas_call x1, Pallas kernels: 24.8 us -> 24.4 us  [shards(): pl.pallas_call(functools.partial(kernel, n), out_shape=[jax.ShapeDtypeStr...]
where the time goes in v4:
time: 28.3 us; the launch traced here: 28.1 us
  Pallas kernels  28.1 us (99%)
    pallas_call x1, Pallas kernels, shards(): pl.pallas_call(functools.partial(kernel, n), out_shape=[jax.ShapeDtypeStr...  24.4 us
    pallas_call x1, Pallas kernels, shards(): pl.pallas_call(correct, out_shape=jax.ShapeDtypeStruct(velocity.shape, f3...  3.72 us

profile of v4, /device:TPU:2, one launch (start us, length us, event | category | flops | bytes accessed | tf_op | source)
XLA Modules:
  0.0 28.1 jit_solution(8209306774675010734)
XLA Ops:
  0.0 24.4 %shard_map.73 = (f32[3,4,128,128]{3,2,1,0:T(8,128)}, f32[6,144,128]{2,1,0:T(8,128)}) custom-call(f32[3,4,128,128]{3,2,1,0:T(8,128)} %vel.1, f32[3,8,128]{2,1,0:T(8,128)} %inflow.1, f32[3,192]{1,0:T(4,128)} %motion.1, f32[3,192]{1,0:T(4,128)} %axis.1, f32[1,192]{1,0:T(1,128)} %bitcast.2, s32[1,192]{1,0:T(1,128)} %bitcast.3, f32[3,192]{1,0:T(4,128)} %frac.1), custom_call_target="tpu_custom_call" | custom-call | tf_op jit(solution)/shard_map/pallas_call | solution.py:573
  24.4 3.7 %shard_map.74 = f32[3,4,128,128]{3,2,1,0:T(8,128)} custom-call(f32[3,4,128,128]{3,2,1,0:T(8,128)} %get-tuple-element.7.given, f32[6,144,128]{2,1,0:T(8,128)} %get-tuple-element.8.below.here.above, f32[6,144,128]{2,1,0:T(8,128)} %get-tuple-element.8.below.here.above, f32[6,144,128]{2,1,0:T(8,128)} %get-tuple-element.8.below.here.above), custom_call_target="tpu_custom_call" | custom-call | tf_op jit(solution)/shard_map/pallas_call | solution.py:630

commit v5 on v3

--- a/solution.py
+++ b/solution.py
@@ -42,7 +42,6 @@
     chord,
     cell,
     frac,
-    given,
     change,
     motion_in,
     axis_in,
@@ -76,7 +75,6 @@
     rim_send,
     rim_recv,
     result,
-    keep_sem,
     store_sem,
 ):
     me = lax.axis_index("gx")
@@ -286,10 +284,6 @@
     def _():
         halo(True).wait_recv()
 
-    @pl.when(has_high)
-    def _():
-        halo(False).wait_recv()
-
     @pl.when(jnp.logical_not(has_low))
     def _():
         def take_inlet(k, carry):
@@ -308,7 +302,6 @@
 
     for i in range(3):
         wrap(u, i, 0)
-        wrap(u, i, cx + 1)
 
     def layer_of(up):
         return pltpu.make_async_remote_copy(
@@ -326,6 +319,12 @@
     def _():
         layer_of(False).start()
 
+    @pl.when(has_high)
+    def _():
+        halo(False).wait_recv()
+
+    for i in range(3):
+        wrap(u, i, cx + 1)
     viscosity(cx, cx - 1, cx, cx + 1)
 
     @pl.when(has_high)
@@ -475,8 +474,6 @@
     first_potential(cx - 2)
     send_rim(False, 3)
     send_rim(True, 3)
-    keep = pltpu.make_async_copy(prov.at[:, 1 : 1 + cx, body], given, keep_sem)
-    keep.start()
     for p in range(1, cx - 1):
         wrap(p1, p + 3)
 
@@ -526,9 +523,9 @@
         for s in starts:
             o = pl.ds(s - PAD, ROWS)
             centre = p3[p + 1, at(s)]
-            result[0, p, o] = 0.5 * (p3[p + 2, at(s)] - p3[p, at(s)])
-            result[1, p, o] = 0.5 * (p3[p + 1, at(s, 1)] - p3[p + 1, at(s, -1)])
-            result[2, p, o] = 0.5 * (deeper(centre) - shallower(centre))
+            result[0, p, o] = prov[0, p + 1, at(s)] - 0.5 * (p3[p + 2, at(s)] - p3[p, at(s)])
+            result[1, p, o] = prov[1, p + 1, at(s)] - 0.5 * (p3[p + 1, at(s, 1)] - p3[p + 1, at(s, -1)])
+            result[2, p, o] = prov[2, p + 1, at(s)] - 0.5 * (deeper(centre) - shallower(centre))
         store(p).start()
         return carry
 
@@ -539,7 +536,6 @@
         return carry
 
     lax.fori_loop(1, n, sent_blade, 0)
-    keep.wait()
     for p in range(cx):
         store(p).wait()
 
@@ -566,11 +562,11 @@
     vmem = pltpu.VMEM
     f32 = jnp.float32
     dma = pltpu.SemaphoreType.DMA
-    provisional, gradient = pl.pallas_call(
+    return pl.pallas_call(
         functools.partial(kernel, n),
-        out_shape=[jax.ShapeDtypeStruct(velocity.shape, f32)] * 2,
+        out_shape=jax.ShapeDtypeStruct(velocity.shape, f32),
         in_specs=[pl.BlockSpec(memory_space=pltpu.HBM)] * 7,
-        out_specs=[pl.BlockSpec(memory_space=pltpu.HBM)] * 2,
+        out_specs=pl.BlockSpec(memory_space=pltpu.HBM),
         scratch_shapes=[
             vmem((3, slots), f32),
             vmem((3, slots), f32),
@@ -604,7 +600,6 @@
             dma((8,)),
             dma((8,)),
             vmem(velocity.shape, f32),
-            dma,
             dma((cx,)),
         ],
         compiler_params=pltpu.CompilerParams(
@@ -619,7 +614,6 @@
         host_cell.reshape(1, slots),
         host_frac,
     )
-    return provisional - gradient
 
 
 def solution(mesh):

time: 27.4 us -> 27.1 us (0.989)
  other arithmetic: 2.33 us -> 0 us
  local copies, waits for them, and re-layouts: 0 us -> 2.06 us
    sub x1 -> x0, other arithmetic: 2.33 us -> none  [shards(): return provisional - gradient]
    unnamed x0 -> x1, local copies, waits for them, and re-layouts: none -> 2.06 us
where the time goes in v5:
time: 27.1 us; the launch traced here: 26.8 us
  Pallas kernels  24.8 us (92%)
  local copies, waits for them, and re-layouts  2.06 us (8%)
    pallas_call x1, Pallas kernels, shards(): pl.pallas_call(functools.partial(kernel, n), out_shape=jax.ShapeDtypeStru...  24.8 us
    unnamed x1, local copies, waits for them, and re-layouts  2.06 us

profile of v5, /device:TPU:2, one launch (start us, length us, event | category | flops | bytes accessed | tf_op | source)
XLA Modules:
  0.0 26.8 jit_solution(1481236673772940014)
XLA Ops:
  0.0 24.8 %shard_map.73 = f32[3,4,128,128]{3,2,1,0:T(8,128)} custom-call(f32[3,4,128,128]{3,2,1,0:T(8,128)} %vel.1, f32[3,8,128]{2,1,0:T(8,128)} %inflow.1, f32[3,192]{1,0:T(4,128)} %motion.1, f32[3,192]{1,0:T(4,128)} %axis.1, f32[1,192]{1,0:T(1,128)} %bitcast.2, s32[1,192]{1,0:T(1,128)} %bitcast.3, f32[3,192]{1,0:T(4,128)} %frac.1), custom_call_target="tpu_custom_call" | custom-call | tf_op jit(solution)/shard_map/pallas_call | solution.py:565
  24.8 2.1 %copy.9 = f32[3,4,128,128]{3,2,1,0:T(8,128)} copy(f32[3,4,128,128]{3,2,1,0:T(8,128)} %shard_map.73) | data formatting | bytes 1572864
